TPU v7x, 768 devices: a whole 4x8x12 slice. The times are simulated.
768 devices in a mesh: dp: 64 (over z_hi, y, x), node: 12 (over z_lo, core).
Axes of the slice: x: 4, y: 8, z: 12 (z_hi: 2, z_lo: 6; z = z_hi * 6 + z_lo), core: 2. Of those that a mesh axis runs over, the one named last changes fastest.
Arguments:
- tokens: bfloat16 [98304, 4096], P(('dp', 'node')), may hold values from -6 to 6
- cotangent: bfloat16 [98304, 512], P(('dp', 'node')), may hold values from -6 to 6
- prim_values: bfloat16 [16896, 128], P(('dp', 'node')), may hold values from -0.09375 to 0.09375
- prim_scales: float32 [16896], P(('dp', 'node')), may hold values from 0.5 to 2
- sec_values: bfloat16 [4104, 512], P('node'), may hold values from -0.09375 to 0.09375
- sec_scales: float32 [4104], P('node'), may hold values from 0.5 to 2
Outputs:
- keys: bfloat16 [98304, 512], P(('dp', 'node'))
- input_grad: bfloat16 [98304, 4096], P(('dp', 'node'))
- weight_grad: float32 [16896, 128], P(('dp', 'node'))
All inputs are finite; a program needn't handle non-finite values.
Results may differ from a plain program's by a relative error of at most 0.019.
Values may be sent and summed in bfloat16 or wider, within the bound.
A program may use at most 64 MiB of HBM per device.

v0:
```python
import jax
import jax.numpy as jnp
from jax import lax
from jax.sharding import PartitionSpec as P

D = 4096
F = 512


def dequantize(values, scales):
    blocks = D * F // 128
    rows = values[:blocks].astype(jnp.float32) * scales[:blocks][:, None]
    return rows.astype(jnp.bfloat16).reshape(D, F)


def scale_rows(values, scales):
    return (values.astype(jnp.float32) * scales[:, None]).astype(jnp.bfloat16)


def local(tokens, cotangent, prim_values, prim_scales, sec_values, sec_scales):
    all_vals, all_scales = (
        lax.all_gather(prim_values, ("dp", "node"), axis=0, tiled=True),
        lax.all_gather(prim_scales.astype(jnp.bfloat16), ("dp", "node"), axis=0, tiled=True).astype(
            prim_scales.dtype
        ),
    )
    w_fwd = dequantize(all_vals, all_scales)
    keys = jnp.dot(tokens, w_fwd, preferred_element_type=jnp.float32).astype(jnp.bfloat16)
    grad_term = lax.dot_general(
        tokens, cotangent, (((0,), (0,)), ((), ())), preferred_element_type=jnp.float32
    )
    grad_term = grad_term.astype(jnp.bfloat16).astype(jnp.float32)
    count_dp = lax.axis_size("dp")
    count_node = lax.axis_size("node")
    per_dev = prim_values.shape[0]
    blocks = D * F // 128
    flat = grad_term.reshape(blocks, 128)
    padding = jnp.zeros((per_dev * count_dp * count_node - blocks, 128), jnp.float32)
    padded = jnp.concatenate([flat, padding], axis=0)
    sec_vals, sec_scls = (
        lax.all_gather(sec_values, "node", axis=0, tiled=True),
        lax.all_gather(sec_scales.astype(jnp.bfloat16), "node", axis=0, tiled=True).astype(
            sec_scales.dtype
        ),
    )
    w_bwd = scale_rows(sec_vals[:D], sec_scls[:D])
    input_grad = lax.dot_general(
        cotangent, w_bwd, (((1,), (1,)), ((), ())), preferred_element_type=jnp.float32
    ).astype(jnp.bfloat16)
    sectioned_in = padded.reshape(count_dp, count_node * per_dev, 128)
    node_sums = lax.psum_scatter(
        sectioned_in.astype(jnp.bfloat16), "node", scatter_dimension=1, tiled=True
    ).astype(jnp.float32)
    summed = lax.psum_scatter(node_sums, "dp", scatter_dimension=0, tiled=True)
    total_tokens = tokens.shape[0] * count_dp * count_node
    weight_grad = summed.reshape(per_dev, 128) * (1.0 / jnp.sqrt(jnp.float32(total_tokens)))
    return (keys, input_grad, weight_grad)


def solution(mesh):
    return jax.shard_map(
        local,
        mesh=mesh,
        in_specs=(
            P(("dp", "node"), None),
            P(("dp", "node"), None),
            P(("dp", "node"), None),
            P(("dp", "node")),
            P("node", None),
            P("node"),
        ),
        out_specs=(P(("dp", "node"), None), P(("dp", "node"), None), P(("dp", "node"), None)),
        check_vma=False,
    )
```

profile of v0, /device:TPU:1, one launch (start us, length us, event | category | flops | bytes accessed | tf_op | source)
XLA Modules:
  0.0 2264.6 jit_solution(11453877296047265553)
XLA Ops:
  7.2 0.0 copy-start
  7.2 0.0 all-gather.7.cloned.1.call-start
  7.2 0.7 all-gather.7.cloned.1.call-update
  7.9 0.0 all-gather.5.cloned.1.call-start
  8.0 0.7 all-gather.5.cloned.1.call-update
  8.7 0.0 reduce-scatter.5.cloned.1.call-start
  8.7 0.0 copy-done
  8.7 4.2 convolution_convert_fusion
  12.9 7.5 reshape.21
  20.4 3.0 concatenate.3
  23.5 3.3 copy.16
  26.8 0.0 copy-start.3
  26.8 0.0 copy-start.2
  26.8 0.0 reduce-scatter.5.cloned.1.call-update
  26.8 0.0 reduce-scatter.7.cloned.1.call-start
  26.8 0.6 copy-done.3
  27.4 1.3 dynamic-slice
  28.7 0.0 copy-done.2
  29.4 0.2 dynamic-update-slice
  29.6 0.2 dynamic-update-slice.1
  29.8 61.4 %all-reduce.2 = bf16[4104]{0:T(1024)(128)(2,1)S(1)} all-reduce(bf16[4104]{0:T(1024)(128)(2,1)S(1)} %dynamic-update-slice.1), channel_id=1, replica_groups=mesh['dp'=64,'node'=12] {'node'}, use_global_device_ids=true, to_apply=%add.2 | all-reduce | flops 4104 | bytes 16416
  91.2 115.1 %all-reduce.1 = bf16[16896]{0:T(1024)(128)(2,1)S(1)} all-reduce(bf16[16896]{0:T(1024)(128)(2,1)S(1)} %dynamic-update-slice), channel_id=1, replica_groups=mesh['dp'=64,'node'=12] {'dp','node'}, use_global_device_ids=true, to_apply=%add.1 | all-reduce | flops 16896 | bytes 67584
  206.3 0.0 copy-start.1
  206.3 0.0 all-gather.7.cloned.1.call-done
  206.4 5.6 reshape.30
  212.0 0.0 copy-done.1
  212.0 3.5 fusion
  215.5 1.3 copy.19
  216.8 1072.3 %all-gather.5.cloned.1.call-done = bf16[768,22,128]{2,1,0:T(8,128)(2,1)} async-done(((bf16[1,22,128]{2,1,0:T(8,128)(2,1)}), bf16[768,22,128]{2,1,0:T(8,128)(2,1)}) %all-gather.5.cloned.1.call-update) | async-done | bytes 4325392 | tf_op jit(solution)/shard_map/all_gather | solution.py:22
  1289.1 7.6 reshape.28
  1296.6 85.2 %reduce-scatter.5.cloned.1.call-done = bf16[64,22,128]{2,0,1:T(8,128)(2,1)} async-done(((bf16[64,264,128]{2,0,1:T(8,128)(2,1)}), bf16[64,22,128]{2,0,1:T(8,128)(2,1)}) %reduce-scatter.5.cloned.1.call-update) | async-done | bytes 360464 | tf_op jit(solution)/shard_map/reduce_scatter | solution.py:51
  1381.9 2.1 copy.17
  1384.0 0.0 reduce-scatter.7.cloned.1.call-update
  1384.0 5.8 multiply_convert_fusion.1
  1389.8 7.6 reshape.20
  1397.4 3.5 fusion.3
  1400.9 0.8 copy.18
  1401.7 855.1 %reduce-scatter.7.cloned.1.call-done = f32[1,22,128]{2,1,0:T(8,128)} async-done(((f32[64,22,128]{2,1,0:T(8,128)}), f32[1,22,128]{2,1,0:T(8,128)}) %reduce-scatter.7.cloned.1.call-update) | async-done | bytes 11280
  2256.7 1.3 multiply_bitcast_fusion
  (6 shorter events, 0.0 us)
Async XLA Ops:
  7.2 1.5 copy-start
  7.2 199.2 %all-gather.7.cloned.1.call-start = ((), (), s32[]{:S(2)}) async-start(), calls=%async_computation.4 | async-start | bytes 4579328 | tf_op jit(solution)/shard_map/all_gather | solution.py:41
  7.9 1281.1 %all-gather.5.cloned.1.call-start = ((), (), s32[]{:S(2)}) async-start(), calls=%async_computation.3 | async-start | bytes 4724736 | tf_op jit(solution)/shard_map/all_gather | solution.py:22
  8.7 1373.2 %reduce-scatter.5.cloned.1.call-start = ((), (), s32[]{:S(2)}) async-start(), calls=%async_computation.2 | async-start | bytes 4685824 | tf_op jit(solution)/shard_map/reduce_scatter | solution.py:51
  26.8 0.7 copy-start.3
  26.8 1.9 copy-start.2
  26.8 2230.0 %reduce-scatter.7.cloned.1.call-start = ((), (), s32[]{:S(2)}) async-start(), calls=%async_computation.5 | async-start | bytes 798720
  206.3 5.6 copy-start.1
Sparse Core Ops, SparseCore 0:
  10.4 83.1 all-gather.6
  96.2 1192.8 all-gather.4
  1292.2 89.5 reduce-scatter.4
  1388.1 868.5 reduce-scatter.6
where the time goes:
time: 2270 us; the launch traced here: 2260 us
  waiting for transfers between devices  2010 us (89%)
  blocking collectives  176 us (8%)
  local copies, waits for them, and re-layouts  41.1 us (2%)
    all_gather x1, waiting for transfers between devices, local(): lax.all_gather(prim_values, ('dp', 'node'), axis=0, tiled=True)  1070 us
    unnamed x5, waiting for transfers between devices  856 us
    unnamed x2, blocking collectives  176 us
    reduce_scatter x1, waiting for transfers between devices, local(): lax.psum_scatter(sectioned_in.astype(jnp.bfloat16), 'node', scatter_dimen...  85.2 us
  transfers between devices with their start and end apart: 4, of which 3 were waited for; matrix products, arithmetic and copies ran while one was open for 2% of the time, Pallas kernels for 0%

commit v1 on v0

v1 whole, which is shorter than its diff:
```python
import jax
import jax.numpy as jnp
from jax import lax
from jax.experimental import pallas as pl
from jax.experimental.pallas import tpu as pltpu
from jax.sharding import PartitionSpec as P

MESH = pl.DeviceIdType.MESH
BF = jnp.bfloat16
F32 = jnp.float32

NX, NY, NZ = 4, 8, 12
ROWS = 144
HALF = 256
SLAB = NX * ROWS
SEC = 368
SEC_A = 192
DEPTHS = (2, 2, 1)


def iota(shape, axis):
    return lax.broadcasted_iota(jnp.int32, shape, axis)


def one_hot(hit):
    return jnp.where(hit, 1.0, 0.0).astype(BF)


def line_of(k, half):
    z, core, h, i = k // 32, (k // 16) % 2, (k // 8) % 2, k % 8
    return jnp.where((i < 6) & (h == half), 11 * z + 5 * core + i, -1)


def dot(a, b):
    return jnp.dot(a, b, preferred_element_type=F32)


def kernel(
    tok, cot, wp, ws, keys, igrad, wgrad,
    te, wf, wst, gs, gr, gx, xr1, xr2, gy, yr, pz, pr, qz, qr, acc, wn,
    pz_s, pz_r, px_s, px_r, py_s, py_r, pc_s, pc_r,
    sz_s, sz_r, sc_s, sc_r,
    gc_s, gc_r, gx_s, gx_r, gy_s, gy_r, gz_s, gz_r,
):
    dp, nd = lax.axis_index("dp"), lax.axis_index("node")
    x, y, z, c = dp % 4, (dp // 4) % 8, (dp // 32) * 6 + nd // 2, nd % 2
    o = 1 - c
    zl = nd // 2

    def dev(dx=0, dy=0, dz=0, core=None):
        xx, yy, zz = (x + dx) % NX, (y + dy) % NY, (z + dz) % NZ
        return ((zz // 6) * 32 + yy * 4 + xx, (zz % 6) * 2 + (c if core is None else core))

    sent = []

    def copy(src, dst, ssem, rsem, target):
        return pltpu.make_async_remote_copy(
            src_ref=src, dst_ref=dst, send_sem=ssem, recv_sem=rsem,
            device_id=target, device_id_type=MESH,
        )

    def send(src, dst, ssem, rsem, target):
        one = copy(src, dst, ssem, rsem, target)
        one.start()
        sent.append(one)

    def landed(dst, ssem, rsem):
        copy(dst, dst, ssem, rsem, dev(core=o)).wait_recv()

    z_partners = [(d, rel) for d in range(NZ) for rel in (0, 1) if (d, rel) != (0, 0)]
    z_partners.sort(key=lambda t: -min(t[0], NZ - t[0]))

    barrier = pltpu.get_barrier_semaphore()
    count = 0
    for d, rel in z_partners:
        pl.semaphore_signal(barrier, inc=1, device_id=dev(dz=d, core=o if rel else c), device_id_type=MESH)
        count += 1
    for d in range(1, NX):
        pl.semaphore_signal(barrier, inc=1, device_id=dev(dx=d), device_id_type=MESH)
        count += 1
    for d in range(1, NY):
        pl.semaphore_signal(barrier, inc=1, device_id=dev(dy=d), device_id_type=MESH)
        count += 1

    k = iota((32, 32), 0)
    want = 4 * (k % 8) + 2 * (k // 16) + (k // 8) % 2 - 2 * c
    keep = (k % 8 < 6) & (want >= 0) & (want < 22)
    pick = one_hot(keep & (iota((32, 32), 1) == want))
    pz[...] = dot(pick, wp[...]).astype(BF).reshape(2, 16, 128)
    wst[nd] = ws[...]

    pl.semaphore_wait(barrier, count)

    for d, rel in z_partners:
        to = o if rel else c
        at = d * 2 + rel
        send(pz.at[to], pr.at[z, c], pz_s.at[at], pz_r.at[at], dev(dz=d, core=to))
    pr[z, c] = pz[c]

    def sec_part(n, piece):
        return wst.at[n, pl.ds(0, SEC_A)] if piece == 0 else wst.at[n, pl.ds(SEC_A, SEC - SEC_A)]

    def sec_node(side, hop):
        return ((zl - hop + 6) % 6 if side == 0 else (zl + hop) % 6) * 2

    def sec_index(side, hop, piece):
        return side * 6 + (hop - 1) * 2 + piece

    def sec_send(side, hop, piece):
        part = sec_part(sec_node(side, hop - 1) + c, piece)
        at = sec_index(side, hop, piece)
        send(part, part, sz_s.at[at], sz_r.at[at], dev(dz=1 if side == 0 else -1 + NZ))

    def sec_cross(side, hop, piece):
        part = sec_part(sec_node(side, hop) + c, piece)
        at = sec_index(side, hop, piece) if hop else 12 + piece
        send(part, part, sc_s.at[at], sc_r.at[at], dev(core=o))

    def sec_arrive(hop, order):
        for side in (0, 1):
            piece = side ^ order
            at = sec_index(side, hop, piece)
            landed(sec_part(sec_node(side, hop) + c, piece), sz_s.at[at], sz_r.at[at])
            if hop == 1 or (hop == 2 and order == 0):
                sec_send(side, hop + 1, piece)
            sec_cross(side, hop, piece)

    for order in (0, 1):
        for side in (0, 1):
            sec_send(side, 1, side ^ order)
    for piece in (0, 1):
        sec_cross(0, 0, piece)

    d = iota((1, SLAB), 1)
    xx = (d >= ROWS).astype(jnp.int32) + (d >= 2 * ROWS).astype(jnp.int32) + (d >= 3 * ROWS).astype(jnp.int32)
    j = d - ROWS * xx
    low = jnp.where(j < 66, 66 * xx + j, -100000)
    high = jnp.where((j >= 66) & (j < 132), 66 * xx + j - 66, -100000)
    for yy in range(NY):
        total = None
        for start, base in ((264 * yy, low), (2112 + 264 * yy, high)):
            a = start // 128 * 128
            wide = min(384, 4096 - a)
            sel = one_hot(iota((wide, SLAB), 0) == base + (start - a))
            part = dot(tok[:, a:a + wide], sel)
            total = part if total is None else total + part
        te[yy] = total.astype(BF)

    for d, rel in z_partners:
        at = d * 2 + rel
        landed(pr.at[(z - d + NZ) % NZ, o if rel else c], pz_s.at[at], pz_r.at[at])
    packets = pr[...].reshape(NZ * 32, 128)
    k = iota((ROWS, NZ * 32), 1)
    r = iota((ROWS, NZ * 32), 0)
    for h in (0, 1):
        wf[c, y, x, :, 128 * h:128 * h + 128] = dot(one_hot(line_of(k, h) == r), packets).astype(BF)
    for d in range(1, NX):
        own = wf.at[c, y, x]
        send(own, own, px_s.at[d], px_r.at[d], dev(dx=d))

    def grad(yy, core):
        part = cot[:, pl.ds(pl.multiple_of(core * HALF, HALF), HALF)]
        out = lax.dot_general(te[yy], part, (((0,), (0,)), ((), ())), preferred_element_type=F32)
        return out.reshape(NX, ROWS, HALF)

    def pair(ref, p):
        return ref.at[:, pl.ds(2 * p, 2)]

    ORDER = (0, 2, 1, 3)
    for p in ORDER:
        for yy in (2 * p, 2 * p + 1):
            gs[:, yy] = grad(yy, o).astype(BF)
        send(pair(gs, p), pair(gr, p), gc_s.at[p], gc_r.at[p], dev(core=o))

    def pri_part(core, side, hop, piece):
        yy = (y - hop + NY) % NY if side == 0 else (y + hop) % NY
        return wf.at[core, yy, pl.ds(2 * piece, 2)]

    def pri_send(side, hop, piece):
        part = pri_part(c, side, hop - 1, piece)
        at = side * 8 + (hop - 1) * 2 + piece
        send(part, part, py_s.at[at], py_r.at[at], dev(dy=1 if side == 0 else NY - 1))

    def pri_cross_at(side, hop, piece):
        return side * 8 + (hop - 1) * 2 + piece if hop else 16 + piece

    def pri_cross(side, hop, piece):
        part = pri_part(c, side, hop, piece)
        at = pri_cross_at(side, hop, piece)
        send(part, part, pc_s.at[at], pc_r.at[at], dev(core=o))

    def pri_arrive(hop, order):
        for side in (0, 1):
            piece = side ^ order
            at = side * 8 + (hop - 1) * 2 + piece
            landed(pri_part(c, side, hop, piece), py_s.at[at], py_r.at[at])
            if hop < 3 or (hop == 3 and order == 0):
                pri_send(side, hop + 1, piece)
            pri_cross(side, hop, piece)

    for d in range(1, NX):
        landed(wf.at[c, y, (x - d + NX) % NX], px_s.at[d], px_r.at[d])
    for order in (0, 1):
        for side in (0, 1):
            pri_send(side, 1, side ^ order)
    for piece in (0, 1):
        pri_cross(0, 0, piece)

    def x_send(side, stage, p):
        far = (x + 2) % NX
        near = (x + 1) % NX if side == 0 else (x + NX - 1) % NX
        src = gx.at[far if stage == 0 else near, pl.ds(2 * p, 2)]
        dst = xr1.at[side, pl.ds(2 * (p % 2), 2)] if stage == 0 else xr2.at[side, pl.ds(2 * p, 2)]
        at = side * 6 + (p % 2 if stage == 0 else 2 + p)
        send(src, dst, gx_s.at[at], gx_r.at[at], dev(dx=1 if side == 0 else NX - 1))

    def x_turn(p):
        side = p // 2
        at = side * 6 + p % 2
        landed(xr1.at[side, pl.ds(2 * (p % 2), 2)], gx_s.at[at], gx_r.at[at])
        near = (x + 1) % NX if side == 0 else (x + NX - 1) % NX
        for yy in (0, 1):
            gx[near, 2 * p + yy] = (
                gx[near, 2 * p + yy].astype(F32) + xr1[side, 2 * (p % 2) + yy].astype(F32)
            ).astype(BF)
        x_send(side, 1, p)

    def own_half(p):
        mine = [grad(yy, c) for yy in (2 * p, 2 * p + 1)]
        landed(pair(gr, p), gc_s.at[p], gc_r.at[p])
        for i in (0, 1):
            yy = 2 * p + i
            gx[:, yy] = (mine[i] + gr[:, yy].astype(F32)).astype(BF)
        side = p // 2
        x_send(side, 0, p)
        x_send(1 - side, 1, p)

    own_half(0)
    sec_arrive(1, 0)
    own_half(2)
    own_half(1)
    sec_arrive(1, 1)
    own_half(3)
    pri_arrive(1, 0)
    x_turn(0)
    x_turn(2)
    sec_arrive(2, 0)
    pri_arrive(1, 1)
    x_turn(1)
    x_turn(3)
    sec_arrive(2, 1)
    pri_arrive(2, 0)
    pri_arrive(2, 1)
    sec_arrive(3, 0)

    def y_sum(p):
        for side in (0, 1):
            at = side * 6 + 2 + p
            landed(xr2.at[side, pl.ds(2 * p, 2)], gx_s.at[at], gx_r.at[at])
        for yy in (2 * p, 2 * p + 1):
            gy[yy] = (gx[x, yy].astype(F32) + xr2[0, yy].astype(F32) + xr2[1, yy].astype(F32)).astype(BF)

    for p in ORDER:
        y_sum(p)
    for d in (4, 3, 5, 2, 6, 1, 7):
        send(gy.at[(y + d) % NY], yr.at[y], gy_s.at[d], gy_r.at[d], dev(dy=d))
    yr[y] = gy[y]
    pri_arrive(3, 0)
    pri_arrive(3, 1)
    pri_arrive(4, 0)

    for d in range(1, NY):
        landed(yr.at[(y - d + NY) % NY], gy_s.at[d], gy_r.at[d])
    line = yr[0].astype(F32)
    for yy in range(1, NY):
        line = line + yr[yy].astype(F32)
    line = line.astype(BF)
    k = iota((NZ * 32, ROWS), 0)
    r = iota((NZ * 32, ROWS), 1)
    packets = dot(one_hot(line_of(k, 0) == r), line[:, :128]) + dot(one_hot(line_of(k, 1) == r), line[:, 128:])
    qz[...] = packets.astype(BF).reshape(NZ, 2, 16, 128)
    for d, rel in z_partners:
        to = o if rel else c
        at = d * 2 + rel
        send(qz.at[(z + d) % NZ, to], qr.at[z, c], gz_s.at[at], gz_r.at[at], dev(dz=d, core=to))
    qr[z, c] = qz[z, c]

    for piece in (0, 1):
        landed(sec_part(zl * 2 + o, piece), sc_s.at[12 + piece], sc_r.at[12 + piece])
        for hop in (1, 2):
            for side in (0, 1):
                at = sec_index(side, hop, piece)
                landed(sec_part(sec_node(side, hop) + o, piece), sc_s.at[at], sc_r.at[at])
        at = sec_index(piece, 3, piece)
        landed(sec_part(sec_node(piece, 3) + o, piece), sc_s.at[at], sc_r.at[at])

    for t in range(256):
        parts = []
        for n in range(12):
            first = 342 * n // 16
            if 342 * n < 16 * t + 16 and 342 * n + 342 > 16 * t:
                parts.append(wst[n, 16 * (t - first):16 * (t - first) + 16])
        tile = parts[0] if len(parts) == 1 else (parts[0].astype(F32) + parts[1].astype(F32)).astype(BF)
        wn[16 * t:16 * t + 16] = tile
    for i in range(8):
        igrad[:, 512 * i:512 * i + 512] = lax.dot_general(
            cot[...], wn[512 * i:512 * i + 512], (((1,), (1,)), ((), ())), preferred_element_type=F32
        ).astype(BF)

    for piece in (0, 1):
        at = 16 + piece
        landed(pri_part(o, 0, 0, piece), pc_s.at[at], pc_r.at[at])
        for side in (0, 1):
            for hop in (1, 2, 3):
                at = pri_cross_at(side, hop, piece)
                landed(pri_part(o, side, hop, piece), pc_s.at[at], pc_r.at[at])
        at = pri_cross_at(piece, 4, piece)
        landed(pri_part(o, piece, 4, piece), pc_s.at[at], pc_r.at[at])
    for core in (0, 1):
        total = None
        for yy in range(NY):
            part = dot(te[yy], wf[core, yy].reshape(SLAB, HALF))
            total = part if total is None else total + part
        keys[:, HALF * core:HALF * core + HALF] = total.astype(BF)

    for d, rel in z_partners:
        at = d * 2 + rel
        landed(qr.at[(z - d + NZ) % NZ, o if rel else c], gz_s.at[at], gz_r.at[at])
    total = qr[0].astype(F32)
    for zz in range(1, NZ):
        total = total + qr[zz].astype(F32)
    total = total.reshape(32, 128)
    k = iota((24, 32), 1)
    want = 4 * (k % 8) + 2 * (k // 16) + (k // 8) % 2 - 2 * c
    pick = jnp.where((k % 8 < 6) & (iota((24, 32), 0) == want), 1.0, 0.0)
    acc[...] = lax.dot_general(
        pick, total, (((1,), (0,)), ((), ())), preferred_element_type=F32, precision=lax.Precision.HIGHEST
    )
    scale = 1.0 / jnp.sqrt(F32(128 * NX * NY * NZ * 2))
    wgrad[...] = acc[:22] * scale

    for one in sent:
        one.wait_send()


def local(tokens, cotangent, prim_values, prim_scales, sec_values, sec_scales):
    wp = (prim_values.astype(F32) * prim_scales[:, None]).astype(BF)
    wp = jnp.pad(wp, ((0, 10), (0, 0)))
    ws = (sec_values.astype(F32) * sec_scales[:, None]).astype(BF)
    shift = (6 * lax.axis_index("node")) % 16
    ws = lax.dynamic_update_slice(jnp.zeros((SEC, 512), BF), ws, (shift, 0))
    dma = pltpu.SemaphoreType.DMA
    vmem = pl.BlockSpec(memory_space=pltpu.VMEM)
    groups = [24, 4, 16, 18, 12, 14, 4, 12, 8, 24]
    return pl.pallas_call(
        kernel,
        name="sharded_projection",
        out_shape=(
            jax.ShapeDtypeStruct((128, 512), BF),
            jax.ShapeDtypeStruct((128, 4096), BF),
            jax.ShapeDtypeStruct((22, 128), F32),
        ),
        in_specs=[vmem] * 4,
        out_specs=(vmem, vmem, vmem),
        scratch_shapes=[
            pltpu.VMEM((NY, 128, SLAB), BF),
            pltpu.VMEM((2, NY, NX, ROWS, HALF), BF),
            pltpu.VMEM((12, SEC, 512), BF),
            pltpu.VMEM((NX, NY, ROWS, HALF), BF),
            pltpu.VMEM((NX, NY, ROWS, HALF), BF),
            pltpu.VMEM((NX, NY, ROWS, HALF), BF),
            pltpu.VMEM((2, 4, ROWS, HALF), BF),
            pltpu.VMEM((2, NY, ROWS, HALF), BF),
            pltpu.VMEM((NY, ROWS, HALF), BF),
            pltpu.VMEM((NY, ROWS, HALF), BF),
            pltpu.VMEM((2, 16, 128), BF),
            pltpu.VMEM((NZ, 2, 16, 128), BF),
            pltpu.VMEM((NZ, 2, 16, 128), BF),
            pltpu.VMEM((NZ, 2, 16, 128), BF),
            pltpu.VMEM((24, 128), F32),
            pltpu.VMEM((4096, 512), BF),
        ]
        + [dma((n,)) for n in groups for _ in (0, 1)],
        compiler_params=pltpu.CompilerParams(
            collective_id=0, has_side_effects=True, vmem_limit_bytes=52 * 2**20
        ),
    )(tokens, cotangent, wp, ws)


def solution(mesh):
    return jax.shard_map(
        local,
        mesh=mesh,
        in_specs=(
            P(("dp", "node"), None),
            P(("dp", "node"), None),
            P(("dp", "node"), None),
            P(("dp", "node")),
            P("node", None),
            P("node"),
        ),
        out_specs=(P(("dp", "node"), None), P(("dp", "node"), None), P(("dp", "node"), None)),
        check_vma=False,
    )
```

time: 2270 us -> 87.2 us (0.04)
  waiting for transfers between devices: 2010 us -> 0 us
  blocking collectives: 176 us -> 0 us
  Pallas kernels: 0 us -> 79.6 us
  local copies, waits for them, and re-layouts: 41.1 us -> 5.49 us
    all_gather x2 -> x0, waiting for transfers between devices: 1070 us -> none  [the longest x1 1070 us: local(): lax.all_gather(prim_values, ('dp', 'node'), axis=0, tiled=True)]
    unnamed x5 -> x0, waiting for transfers between devices: 856 us -> none
    unnamed x2 -> x0, blocking collectives: 176 us -> none
    reduce_scatter x1 -> x0, waiting for transfers between devices: 85.2 us -> none  [local(): lax.psum_scatter(sectioned_in.astype(jnp.bfloat16), 'node', scatter_dimen...]
    pallas_call x0 -> x1, Pallas kernels: none -> 79.6 us  [local(): pl.pallas_call(kernel, name='sharded_projection', out_shape=(jax.ShapeDty...]
  transfers between devices with their start and end apart: 4 -> 0, of which waited for: 3 -> 0; matrix products, arithmetic and copies ran while one was open for 2% -> 0% of each run, Pallas kernels for 0% -> 0%
where the time goes in v1:
time: 87.2 us; the launch traced here: 87 us
  Pallas kernels  79.6 us (91%)
  local copies, waits for them, and re-layouts  5.49 us (6%)
  other arithmetic  1.18 us (1%)
    pallas_call x1, Pallas kernels, local(): pl.pallas_call(kernel, name='sharded_projection', out_shape=(jax.ShapeDty...  79.6 us
    unnamed x11, local copies, waits for them, and re-layouts  3.58 us
    dynamic_update_slice x1, local copies, waits for them, and re-layouts, local(): ws = lax.dynamic_update_slice(jnp.zeros((SEC, 512), BF), ws, (shift, 0))  1.88 us

profile of v1, /device:TPU:1, one launch (start us, length us, event | category | flops | bytes accessed | tf_op | source)
XLA Modules:
  0.0 87.0 jit_solution(8782954401727306347)
XLA Ops:
  0.6 0.0 copy-start.1
  0.7 0.0 copy-start.3
  0.7 0.7 copy-done.1
  1.3 0.0 copy-done.3
  1.3 0.1 multiply_convert_fusion.1
  1.4 0.0 copy-start.2
  1.4 0.7 copy-done.2
  2.1 1.1 %multiply_convert_fusion = bf16[342,512]{1,0:T(8,128)(2,1)S(1)} fusion(bf16[342,512]{1,0:T(8,128)(2,1)} %param.10, f32[342]{0:T(512)S(1)} %copy-done.2), kind=kLoop, calls=%fused_computation | loop fusion | flops 525312 | bytes 701784 | tf_op jit(solution)/shard_map/convert_element_type | solution.py:349
  3.3 0.0 copy-start
  3.3 1.9 %dynamic_update_slice.3.ws = bf16[368,512]{1,0:T(8,128)(2,1)S(1)} dynamic-update-slice(bf16[368,512]{1,0:T(8,128)(2,1)S(1)} %broadcast_in_dim.2, bf16[342,512]{1,0:T(8,128)(2,1)S(1)} %multiply_convert_fusion, s32[]{:T(128)S(6)} %select_n.11, s32[]{:T(128)} %constant.20.clone.1) | dynamic-update-slice | bytes 700420 | tf_op jit(solution)/shard_map/dynamic_update_slice | solution.py:351
  5.2 0.0 copy-done
  5.2 79.6 %sharded_projection.1 = (bf16[128,512]{1,0:T(8,128)(2,1)S(1)}, bf16[128,4096]{1,0:T(8,128)(2,1)S(1)}, f32[22,128]{1,0:T(8,128)S(1)}) custom-call(bf16[128,4096]{1,0:T(8,128)(2,1)} %tok.1, bf16[128,512]{1,0:T(8,128)(2,1)S(1)} %copy-done, bf16[32,128]{1,0:T(8,128)(2,1)S(1)} %pad.4.wp, bf16[368,512]{1,0:T(8,128)(2,1)S(1)} %dynamic_update_slice.3.ws), custom_call_target="tpu_custom_call" | custom-call | tf_op jit(solution)/shard_map/sharded_projection/pallas_call | solution.py:355
  84.7 0.7 copy.13
  85.4 1.0 %copy.14 = bf16[128,4096]{1,0:T(8,128)(2,1)} copy(bf16[128,4096]{1,0:T(8,128)(2,1)S(1)} %get-tuple-element.7) | data formatting | bytes 2097152
  86.4 0.6 copy.15
  (2 shorter events, 0.0 us)
Async XLA Ops:
  0.6 0.7 copy-start.1
  0.7 0.7 copy-start.3
  1.4 0.7 copy-start.2
  3.3 1.9 %copy-start = (bf16[128,512]{1,0:T(8,128)(2,1)S(1)}, bf16[128,512]{1,0:T(8,128)(2,1)}, u32[]{:S(2)}) copy-start(bf16[128,512]{1,0:T(8,128)(2,1)} %cot.1) | copy-start | bytes 393220

commit v2 on v1

--- a/solution.py
+++ b/solution.py
@@ -13,9 +13,11 @@
 ROWS = 144
 HALF = 256
 SLAB = NX * ROWS
+LANES = 128
 SEC = 368
 SEC_A = 192
-DEPTHS = (2, 2, 1)
+RING = (4, 3, 5, 2, 6, 1, 7, 0)
+PLACE = {r: k for k, r in enumerate(RING)}
 
 
 def iota(shape, axis):
@@ -36,11 +38,11 @@
 
 
 def kernel(
-    tok, cot, wp, ws, keys, igrad, wgrad,
-    te, wf, wst, gs, gr, gx, xr1, xr2, gy, yr, pz, pr, qz, qr, acc, wn,
-    pz_s, pz_r, px_s, px_r, py_s, py_r, pc_s, pc_r,
+    tok, cot, pv, ps, sv, sc, keys, igrad, wgrad,
+    te, wf0, wf1, wst, gs, gr, gx0, gx1, xr1, xr2, gy, yr, g1r, hx, xr3, pz, pr, qz, qr, acc, wn,
+    pz_s, pz_r, px_s, px_r, py_s, py_r, pc_s, pc_r, ru_s, ru_r, rx_s, rx_r, rc_s, rc_r,
     sz_s, sz_r, sc_s, sc_r,
-    gc_s, gc_r, gx_s, gx_r, gy_s, gy_r, gz_s, gz_r,
+    gc_s, gc_r, gx_s, gx_r, gy_s, gy_r, hy_s, hy_r, hx_s, hx_r, gz_s, gz_r,
 ):
     dp, nd = lax.axis_index("dp"), lax.axis_index("node")
     x, y, z, c = dp % 4, (dp // 4) % 8, (dp // 32) * 6 + nd // 2, nd % 2
@@ -75,19 +77,18 @@
     for d, rel in z_partners:
         pl.semaphore_signal(barrier, inc=1, device_id=dev(dz=d, core=o if rel else c), device_id_type=MESH)
         count += 1
+    for d in range(1, NY):
+        pl.semaphore_signal(barrier, inc=1, device_id=dev(dy=d), device_id_type=MESH)
+        count += 1
     for d in range(1, NX):
         pl.semaphore_signal(barrier, inc=1, device_id=dev(dx=d), device_id_type=MESH)
         count += 1
-    for d in range(1, NY):
-        pl.semaphore_signal(barrier, inc=1, device_id=dev(dy=d), device_id_type=MESH)
-        count += 1
-
-    k = iota((32, 32), 0)
+
+    k = iota((32, 22), 0)
     want = 4 * (k % 8) + 2 * (k // 16) + (k // 8) % 2 - 2 * c
-    keep = (k % 8 < 6) & (want >= 0) & (want < 22)
-    pick = one_hot(keep & (iota((32, 32), 1) == want))
-    pz[...] = dot(pick, wp[...]).astype(BF).reshape(2, 16, 128)
-    wst[nd] = ws[...]
+    hit = (k % 8 < 6) & (iota((32, 22), 1) == want)
+    factor = jnp.sum(jnp.where(hit, ps[...], 0.0), axis=1, keepdims=True)
+    pz[...] = (dot(one_hot(hit), pv[...]) * factor).astype(BF).reshape(2, 16, 128)
 
     pl.semaphore_wait(barrier, count)
 
@@ -97,6 +98,10 @@
         send(pz.at[to], pr.at[z, c], pz_s.at[at], pz_r.at[at], dev(dz=d, core=to))
     pr[z, c] = pz[c]
 
+    hit = iota((SEC, 342), 1) == iota((SEC, 342), 0) - (6 * nd) % 16
+    factor = jnp.sum(jnp.where(hit, sc[...], 0.0), axis=1, keepdims=True)
+    wst[nd] = (dot(one_hot(hit), sv[...]) * factor).astype(BF)
+
     def sec_part(n, piece):
         return wst.at[n, pl.ds(0, SEC_A)] if piece == 0 else wst.at[n, pl.ds(SEC_A, SEC - SEC_A)]
 
@@ -109,7 +114,7 @@
     def sec_send(side, hop, piece):
         part = sec_part(sec_node(side, hop - 1) + c, piece)
         at = sec_index(side, hop, piece)
-        send(part, part, sz_s.at[at], sz_r.at[at], dev(dz=1 if side == 0 else -1 + NZ))
+        send(part, part, sz_s.at[at], sz_r.at[at], dev(dz=1 if side == 0 else NZ - 1))
 
     def sec_cross(side, hop, piece):
         part = sec_part(sec_node(side, hop) + c, piece)
@@ -128,8 +133,6 @@
     for order in (0, 1):
         for side in (0, 1):
             sec_send(side, 1, side ^ order)
-    for piece in (0, 1):
-        sec_cross(0, 0, piece)
 
     d = iota((1, SLAB), 1)
     xx = (d >= ROWS).astype(jnp.int32) + (d >= 2 * ROWS).astype(jnp.int32) + (d >= 3 * ROWS).astype(jnp.int32)
@@ -146,40 +149,44 @@
             total = part if total is None else total + part
         te[yy] = total.astype(BF)
 
+    def grad(k, core):
+        part = cot[:, pl.ds(pl.multiple_of(core * HALF, HALF), HALF)]
+        rows = te[(y + RING[k]) % NY]
+        out = lax.dot_general(rows, part, (((0,), (0,)), ((), ())), preferred_element_type=F32)
+        return out.reshape(NX, ROWS, HALF)
+
+    def give(k):
+        gs[k] = grad(k, o).astype(BF)
+        send(gs.at[k], gr.at[k], gc_s.at[k], gc_r.at[k], dev(core=o))
+
+    for k in range(4):
+        give(k)
+
     for d, rel in z_partners:
         at = d * 2 + rel
         landed(pr.at[(z - d + NZ) % NZ, o if rel else c], pz_s.at[at], pz_r.at[at])
     packets = pr[...].reshape(NZ * 32, 128)
     k = iota((ROWS, NZ * 32), 1)
     r = iota((ROWS, NZ * 32), 0)
-    for h in (0, 1):
-        wf[c, y, x, :, 128 * h:128 * h + 128] = dot(one_hot(line_of(k, h) == r), packets).astype(BF)
-    for d in range(1, NX):
-        own = wf.at[c, y, x]
+    wf1[c, x, 0] = dot(one_hot(line_of(k, 1) == r), packets).astype(BF)
+    wf0[c, 0, x] = dot(one_hot(line_of(k, 0) == r), packets).astype(BF)
+    for d in (4, 3, 5, 2, 6, 1, 7):
+        send(wf1.at[c, x, 0], wf1.at[c, x, NY - d], ru_s.at[d], ru_r.at[d], dev(dy=d))
+    for d in (2, 1, 3):
+        own = wf0.at[c, 0, x]
         send(own, own, px_s.at[d], px_r.at[d], dev(dx=d))
 
-    def grad(yy, core):
-        part = cot[:, pl.ds(pl.multiple_of(core * HALF, HALF), HALF)]
-        out = lax.dot_general(te[yy], part, (((0,), (0,)), ((), ())), preferred_element_type=F32)
-        return out.reshape(NX, ROWS, HALF)
-
-    def pair(ref, p):
-        return ref.at[:, pl.ds(2 * p, 2)]
-
-    ORDER = (0, 2, 1, 3)
-    for p in ORDER:
-        for yy in (2 * p, 2 * p + 1):
-            gs[:, yy] = grad(yy, o).astype(BF)
-        send(pair(gs, p), pair(gr, p), gc_s.at[p], gc_r.at[p], dev(core=o))
+    for k in range(4, 8):
+        give(k)
+    sec_arrive(1, 0)
 
     def pri_part(core, side, hop, piece):
-        yy = (y - hop + NY) % NY if side == 0 else (y + hop) % NY
-        return wf.at[core, yy, pl.ds(2 * piece, 2)]
+        return wf0.at[core, (NY - hop) % NY if side == 0 else hop, pl.ds(2 * piece, 2)]
 
     def pri_send(side, hop, piece):
-        part = pri_part(c, side, hop - 1, piece)
         at = side * 8 + (hop - 1) * 2 + piece
-        send(part, part, py_s.at[at], py_r.at[at], dev(dy=1 if side == 0 else NY - 1))
+        send(pri_part(c, side, hop - 1, piece), pri_part(c, side, hop, piece),
+             py_s.at[at], py_r.at[at], dev(dy=1 if side == 0 else NY - 1))
 
     def pri_cross_at(side, hop, piece):
         return side * 8 + (hop - 1) * 2 + piece if hop else 16 + piece
@@ -198,86 +205,175 @@
                 pri_send(side, hop + 1, piece)
             pri_cross(side, hop, piece)
 
-    for d in range(1, NX):
-        landed(wf.at[c, y, (x - d + NX) % NX], px_s.at[d], px_r.at[d])
-    for order in (0, 1):
-        for side in (0, 1):
-            pri_send(side, 1, side ^ order)
-    for piece in (0, 1):
-        pri_cross(0, 0, piece)
+    def pri_turn():
+        for d in range(1, NX):
+            landed(wf0.at[c, 0, (x - d + NX) % NX], px_s.at[d], px_r.at[d])
+        for order in (0, 1):
+            for side in (0, 1):
+                pri_send(side, 1, side ^ order)
+        for piece in (0, 1):
+            pri_cross(0, 0, piece)
+
+    def alt_part(core, side, hop, piece):
+        xx = (x - hop + NX) % NX if side == 0 else (x + hop) % NX
+        return wf1.at[core, xx, pl.ds(4 * piece, 4)]
+
+    def alt_send(side, hop, piece):
+        part = alt_part(c, side, hop - 1, piece)
+        at = side * 4 + (hop - 1) * 2 + piece
+        send(part, part, rx_s.at[at], rx_r.at[at], dev(dx=1 if side == 0 else NX - 1))
+
+    def alt_cross_at(side, hop, piece):
+        return side * 4 + (hop - 1) * 2 + piece if hop else 8 + piece
+
+    def alt_cross(side, hop, piece):
+        part = alt_part(c, side, hop, piece)
+        at = alt_cross_at(side, hop, piece)
+        send(part, part, rc_s.at[at], rc_r.at[at], dev(core=o))
+
+    def alt_arrive(hop, order):
+        for side in (0, 1):
+            piece = side ^ order
+            at = side * 4 + (hop - 1) * 2 + piece
+            landed(alt_part(c, side, hop, piece), rx_s.at[at], rx_r.at[at])
+            if hop == 1 and order == 0:
+                alt_send(side, 2, piece)
+            alt_cross(side, hop, piece)
+
+    def alt_turn():
+        for d in range(1, NY):
+            landed(wf1.at[c, x, NY - d], ru_s.at[d], ru_r.at[d])
+        for order in (0, 1):
+            for side in (0, 1):
+                alt_send(side, 1, side ^ order)
+        for piece in (0, 1):
+            alt_cross(0, 0, piece)
 
     def x_send(side, stage, p):
         far = (x + 2) % NX
         near = (x + 1) % NX if side == 0 else (x + NX - 1) % NX
-        src = gx.at[far if stage == 0 else near, pl.ds(2 * p, 2)]
-        dst = xr1.at[side, pl.ds(2 * (p % 2), 2)] if stage == 0 else xr2.at[side, pl.ds(2 * p, 2)]
-        at = side * 6 + (p % 2 if stage == 0 else 2 + p)
+        src = gx0.at[far if stage == 0 else near, pl.ds(2 * p, 2)]
+        dst = xr1.at[side, pl.ds(2 * (p // 2), 2)] if stage == 0 else xr2.at[side, pl.ds(2 * p, 2)]
+        at = side * 6 + (p // 2 if stage == 0 else 2 + p)
         send(src, dst, gx_s.at[at], gx_r.at[at], dev(dx=1 if side == 0 else NX - 1))
 
     def x_turn(p):
-        side = p // 2
-        at = side * 6 + p % 2
-        landed(xr1.at[side, pl.ds(2 * (p % 2), 2)], gx_s.at[at], gx_r.at[at])
+        side = p % 2
+        at = side * 6 + p // 2
+        landed(xr1.at[side, pl.ds(2 * (p // 2), 2)], gx_s.at[at], gx_r.at[at])
         near = (x + 1) % NX if side == 0 else (x + NX - 1) % NX
-        for yy in (0, 1):
-            gx[near, 2 * p + yy] = (
-                gx[near, 2 * p + yy].astype(F32) + xr1[side, 2 * (p % 2) + yy].astype(F32)
+        for i in (0, 1):
+            gx0[near, 2 * p + i] = (
+                gx0[near, 2 * p + i].astype(F32) + xr1[side, 2 * (p // 2) + i].astype(F32)
             ).astype(BF)
         x_send(side, 1, p)
 
+    def y_at(side, hop, piece):
+        return side * 8 + (hop - 1) * 2 + piece
+
+    def y_send(side, hop, piece):
+        src = gx1.at[PLACE[5 - hop if side == 0 else 3 + hop], pl.ds(2 * piece, 2)]
+        at = y_at(side, hop, piece)
+        send(src, g1r.at[side, hop - 1, pl.ds(2 * piece, 2)], hy_s.at[at], hy_r.at[at],
+             dev(dy=1 if side == 0 else NY - 1))
+
+    def y_turn(side, hop, piece):
+        at = y_at(side, hop, piece)
+        part = pl.ds(2 * piece, 2)
+        landed(g1r.at[side, hop - 1, part], hy_s.at[at], hy_r.at[at])
+        k = PLACE[4 - hop if side == 0 else 4 + hop]
+        gx1[k, part] = (gx1[k, part].astype(F32) + g1r[side, hop - 1, part].astype(F32)).astype(BF)
+        y_send(side, hop + 1, piece)
+
     def own_half(p):
-        mine = [grad(yy, c) for yy in (2 * p, 2 * p + 1)]
-        landed(pair(gr, p), gc_s.at[p], gc_r.at[p])
-        for i in (0, 1):
-            yy = 2 * p + i
-            gx[:, yy] = (mine[i] + gr[:, yy].astype(F32)).astype(BF)
-        side = p // 2
+        for k in (2 * p, 2 * p + 1):
+            mine = grad(k, c)
+            landed(gr.at[k], gc_s.at[k], gc_r.at[k])
+            mine = (mine + gr[k].astype(F32)).astype(BF)
+            gx0[:, k] = mine[:, :, :LANES]
+            gx1[k] = mine[:, :, LANES:]
+            if RING[k] == 4:
+                y_send(0, 1, 0)
+                y_send(1, 1, 1)
+            if RING[k] == 3:
+                y_send(0, 2, 1)
+            if RING[k] == 5:
+                y_send(1, 2, 0)
+        side = p % 2
         x_send(side, 0, p)
         x_send(1 - side, 1, p)
 
     own_half(0)
-    sec_arrive(1, 0)
+    own_half(1)
+    pri_turn()
     own_half(2)
-    own_half(1)
+    own_half(3)
     sec_arrive(1, 1)
-    own_half(3)
+    for piece in (0, 1):
+        sec_cross(0, 0, piece)
+    x_turn(0)
+    x_turn(1)
+    y_turn(0, 1, 0)
+    y_turn(1, 1, 1)
+    alt_turn()
     pri_arrive(1, 0)
-    x_turn(0)
+    sec_arrive(2, 0)
+    y_turn(0, 2, 1)
+    y_turn(1, 2, 0)
     x_turn(2)
-    sec_arrive(2, 0)
+    x_turn(3)
     pri_arrive(1, 1)
-    x_turn(1)
-    x_turn(3)
+    y_turn(0, 2, 0)
+    y_turn(1, 2, 1)
+    pri_arrive(2, 0)
+    y_turn(0, 3, 1)
+    y_turn(1, 3, 0)
     sec_arrive(2, 1)
-    pri_arrive(2, 0)
     pri_arrive(2, 1)
-    sec_arrive(3, 0)
-
-    def y_sum(p):
+    alt_arrive(1, 0)
+    y_turn(0, 3, 0)
+    y_turn(1, 3, 1)
+
+    for p in (0, 1, 2, 3):
         for side in (0, 1):
             at = side * 6 + 2 + p
             landed(xr2.at[side, pl.ds(2 * p, 2)], gx_s.at[at], gx_r.at[at])
-        for yy in (2 * p, 2 * p + 1):
-            gy[yy] = (gx[x, yy].astype(F32) + xr2[0, yy].astype(F32) + xr2[1, yy].astype(F32)).astype(BF)
-
-    for p in ORDER:
-        y_sum(p)
-    for d in (4, 3, 5, 2, 6, 1, 7):
-        send(gy.at[(y + d) % NY], yr.at[y], gy_s.at[d], gy_r.at[d], dev(dy=d))
-    yr[y] = gy[y]
+        for k in (2 * p, 2 * p + 1):
+            mine = (gx0[x, k].astype(F32) + xr2[0, k].astype(F32) + xr2[1, k].astype(F32)).astype(BF)
+            if RING[k]:
+                gy[k] = mine
+                send(gy.at[k], yr.at[k], gy_s.at[k], gy_r.at[k], dev(dy=RING[k]))
+            else:
+                yr[k] = mine
     pri_arrive(3, 0)
+    sec_arrive(3, 0)
+
+    for piece in (1, 0):
+        for side in (0, 1):
+            at = y_at(side, 4, piece)
+            landed(g1r.at[side, 3, pl.ds(2 * piece, 2)], hy_s.at[at], hy_r.at[at])
+    hx[...] = (gx1[PLACE[0]].astype(F32) + g1r[0, 3].astype(F32) + g1r[1, 3].astype(F32)).astype(BF)
+    for d in (2, 1, 3):
+        send(hx.at[(x + d) % NX], xr3.at[d], hx_s.at[d], hx_r.at[d], dev(dx=d))
+    xr3[0] = hx[x]
+    alt_arrive(1, 1)
     pri_arrive(3, 1)
+    alt_arrive(2, 0)
     pri_arrive(4, 0)
 
-    for d in range(1, NY):
-        landed(yr.at[(y - d + NY) % NY], gy_s.at[d], gy_r.at[d])
-    line = yr[0].astype(F32)
-    for yy in range(1, NY):
-        line = line + yr[yy].astype(F32)
-    line = line.astype(BF)
+    for k in range(7):
+        landed(yr.at[k], gy_s.at[k], gy_r.at[k])
+    line0 = yr[0].astype(F32)
+    for k in range(1, NY):
+        line0 = line0 + yr[k].astype(F32)
+    for d in range(1, NX):
+        landed(xr3.at[d], hx_s.at[d], hx_r.at[d])
+    line1 = xr3[0].astype(F32)
+    for d in range(1, NX):
+        line1 = line1 + xr3[d].astype(F32)
     k = iota((NZ * 32, ROWS), 0)
     r = iota((NZ * 32, ROWS), 1)
-    packets = dot(one_hot(line_of(k, 0) == r), line[:, :128]) + dot(one_hot(line_of(k, 1) == r), line[:, 128:])
+    packets = dot(one_hot(line_of(k, 0) == r), line0.astype(BF)) + dot(one_hot(line_of(k, 1) == r), line1.astype(BF))
     qz[...] = packets.astype(BF).reshape(NZ, 2, 16, 128)
     for d, rel in z_partners:
         to = o if rel else c
@@ -310,16 +406,23 @@
     for piece in (0, 1):
         at = 16 + piece
         landed(pri_part(o, 0, 0, piece), pc_s.at[at], pc_r.at[at])
+        at = 8 + piece
+        landed(alt_part(o, 0, 0, piece), rc_s.at[at], rc_r.at[at])
         for side in (0, 1):
             for hop in (1, 2, 3):
                 at = pri_cross_at(side, hop, piece)
                 landed(pri_part(o, side, hop, piece), pc_s.at[at], pc_r.at[at])
+            at = alt_cross_at(side, 1, piece)
+            landed(alt_part(o, side, 1, piece), rc_s.at[at], rc_r.at[at])
         at = pri_cross_at(piece, 4, piece)
         landed(pri_part(o, piece, 4, piece), pc_s.at[at], pc_r.at[at])
+        at = alt_cross_at(piece, 2, piece)
+        landed(alt_part(o, piece, 2, piece), rc_s.at[at], rc_r.at[at])
     for core in (0, 1):
         total = None
-        for yy in range(NY):
-            part = dot(te[yy], wf[core, yy].reshape(SLAB, HALF))
+        for r in range(NY):
+            w = jnp.concatenate([wf0[core, r].reshape(SLAB, LANES), wf1[core, :, r].reshape(SLAB, LANES)], axis=1)
+            part = dot(te[(y + r) % NY], w)
             total = part if total is None else total + part
         keys[:, HALF * core:HALF * core + HALF] = total.astype(BF)
 
@@ -344,14 +447,9 @@
 
 
 def local(tokens, cotangent, prim_values, prim_scales, sec_values, sec_scales):
-    wp = (prim_values.astype(F32) * prim_scales[:, None]).astype(BF)
-    wp = jnp.pad(wp, ((0, 10), (0, 0)))
-    ws = (sec_values.astype(F32) * sec_scales[:, None]).astype(BF)
-    shift = (6 * lax.axis_index("node")) % 16
-    ws = lax.dynamic_update_slice(jnp.zeros((SEC, 512), BF), ws, (shift, 0))
     dma = pltpu.SemaphoreType.DMA
     vmem = pl.BlockSpec(memory_space=pltpu.VMEM)
-    groups = [24, 4, 16, 18, 12, 14, 4, 12, 8, 24]
+    groups = [24, 4, 16, 18, 8, 8, 10, 12, 14, 8, 12, 8, 16, 4, 24]
     return pl.pallas_call(
         kernel,
         name="sharded_projection",
@@ -360,19 +458,24 @@
             jax.ShapeDtypeStruct((128, 4096), BF),
             jax.ShapeDtypeStruct((22, 128), F32),
         ),
-        in_specs=[vmem] * 4,
+        in_specs=[vmem] * 6,
         out_specs=(vmem, vmem, vmem),
         scratch_shapes=[
             pltpu.VMEM((NY, 128, SLAB), BF),
-            pltpu.VMEM((2, NY, NX, ROWS, HALF), BF),
+            pltpu.VMEM((2, NY, NX, ROWS, LANES), BF),
+            pltpu.VMEM((2, NX, NY, ROWS, LANES), BF),
             pltpu.VMEM((12, SEC, 512), BF),
-            pltpu.VMEM((NX, NY, ROWS, HALF), BF),
-            pltpu.VMEM((NX, NY, ROWS, HALF), BF),
-            pltpu.VMEM((NX, NY, ROWS, HALF), BF),
-            pltpu.VMEM((2, 4, ROWS, HALF), BF),
-            pltpu.VMEM((2, NY, ROWS, HALF), BF),
-            pltpu.VMEM((NY, ROWS, HALF), BF),
-            pltpu.VMEM((NY, ROWS, HALF), BF),
+            pltpu.VMEM((NY, NX, ROWS, HALF), BF),
+            pltpu.VMEM((NY, NX, ROWS, HALF), BF),
+            pltpu.VMEM((NX, NY, ROWS, LANES), BF),
+            pltpu.VMEM((NY, NX, ROWS, LANES), BF),
+            pltpu.VMEM((2, 4, ROWS, LANES), BF),
+            pltpu.VMEM((2, NY, ROWS, LANES), BF),
+            pltpu.VMEM((NY, ROWS, LANES), BF),
+            pltpu.VMEM((NY, ROWS, LANES), BF),
+            pltpu.VMEM((2, 4, NX, ROWS, LANES), BF),
+            pltpu.VMEM((NX, ROWS, LANES), BF),
+            pltpu.VMEM((NX, ROWS, LANES), BF),
             pltpu.VMEM((2, 16, 128), BF),
             pltpu.VMEM((NZ, 2, 16, 128), BF),
             pltpu.VMEM((NZ, 2, 16, 128), BF),
@@ -384,7 +487,7 @@
         compiler_params=pltpu.CompilerParams(
             collective_id=0, has_side_effects=True, vmem_limit_bytes=52 * 2**20
         ),
-    )(tokens, cotangent, wp, ws)
+    )(tokens, cotangent, prim_values, prim_scales.reshape(1, -1), sec_values, sec_scales.reshape(1, -1))
 
 
 def solution(mesh):

time: 87.2 us -> 80.5 us (0.923)
  Pallas kernels: 79.6 us -> 74 us
  other arithmetic: 1.18 us -> 0 us
    pallas_call x1, Pallas kernels: 79.6 us -> 74 us  [local(): pl.pallas_call(kernel, name='sharded_projection', out_shape=(jax.ShapeDty...]
    dynamic_update_slice x1 -> x0, local copies, waits for them, and re-layouts: 1.88 us -> none  [local(): ws = lax.dynamic_update_slice(jnp.zeros((SEC, 512), BF), ws, (shift, 0))]
    unnamed x11, local copies, waits for them, and re-layouts: 3.58 us -> 4.81 us
    convert_element_type x2 -> x0, other arithmetic: 1.18 us -> none  [the longest x1 1.11 us: local(): ws = (sec_values.astype(F32) * sec_scales[:, None]).astype(BF)]
where the time goes in v2:
time: 80.5 us; the launch traced here: 80.2 us
  Pallas kernels  74 us (92%)
  local copies, waits for them, and re-layouts  5.5 us (7%)
    pallas_call x1, Pallas kernels, local(): pl.pallas_call(kernel, name='sharded_projection', out_shape=(jax.ShapeDty...  74 us
    unnamed x11, local copies, waits for them, and re-layouts  4.81 us

profile of v2, /device:TPU:1, one launch (start us, length us, event | category | flops | bytes accessed | tf_op | source)
XLA Modules:
  0.0 80.2 jit_solution(10255631136934768100)
XLA Ops:
  0.6 0.0 copy-start.3
  0.6 0.7 reshape.13.sc
  1.3 0.0 copy-done.3
  1.3 0.0 copy-start
  1.3 1.0 %copy-done = bf16[342,512]{1,0:T(8,128)(2,1)S(1)} copy-done((bf16[342,512]{1,0:T(8,128)(2,1)S(1)}, bf16[342,512]{1,0:T(8,128)(2,1)}, u32[]{:S(2)}) %copy-start) | copy-done | bytes 350232
  2.3 0.0 copy-start.1
  2.3 0.9 %copy-done.1 = bf16[128,512]{1,0:T(8,128)(2,1)S(1)} copy-done((bf16[128,512]{1,0:T(8,128)(2,1)S(1)}, bf16[128,512]{1,0:T(8,128)(2,1)}, u32[]{:S(2)}) %copy-start.1) | copy-done | bytes 131096
  3.2 0.0 copy-start.2
  3.2 0.7 copy-done.2
  3.9 74.0 %sharded_projection.1 = (bf16[128,512]{1,0:T(8,128)(2,1)S(1)}, bf16[128,4096]{1,0:T(8,128)(2,1)S(1)}, f32[22,128]{1,0:T(8,128)S(1)}) custom-call(bf16[128,4096]{1,0:T(8,128)(2,1)} %tok.1, bf16[128,512]{1,0:T(8,128)(2,1)S(1)} %copy-done.1, bf16[22,128]{1,0:T(8,128)(2,1)S(1)} %copy-done.2, f32[1,22]{1,0:T(1,128)S(1)} %bitcast.1, bf16[342,512]{1,0:T(8,128)(2,1)S(1)} %copy-done, ...), custom_call_target="tpu_custom_call" | custom-call | tf_op jit(solution)/shard_map/sharded_projection/pallas_call | solution.py:453
  78.0 0.7 copy.12
  78.6 1.0 %copy.13 = bf16[128,4096]{1,0:T(8,128)(2,1)} copy(bf16[128,4096]{1,0:T(8,128)(2,1)S(1)} %get-tuple-element.7) | data formatting | bytes 2097152
  79.6 0.6 copy.14
Async XLA Ops:
  0.6 0.7 copy-start.3
  1.3 1.0 %copy-start = (bf16[342,512]{1,0:T(8,128)(2,1)S(1)}, bf16[342,512]{1,0:T(8,128)(2,1)}, u32[]{:S(2)}) copy-start(bf16[342,512]{1,0:T(8,128)(2,1)} %sv.1) | copy-start | bytes 1050628
  2.3 0.9 %copy-start.1 = (bf16[128,512]{1,0:T(8,128)(2,1)S(1)}, bf16[128,512]{1,0:T(8,128)(2,1)}, u32[]{:S(2)}) copy-start(bf16[128,512]{1,0:T(8,128)(2,1)} %cot.1) | copy-start | bytes 393220
  3.2 0.7 copy-start.2

commit v3 on v2

--- a/solution.py
+++ b/solution.py
@@ -13,6 +13,7 @@
 ROWS = 144
 HALF = 256
 SLAB = NX * ROWS
+CUT = 64
 LANES = 128
 SEC = 368
 SEC_A = 192
@@ -38,7 +39,8 @@
 
 
 def kernel(
-    tok, cot, pv, ps, sv, sc, keys, igrad, wgrad,
+    tok_in, cot_in, pv, ps, sv_in, sc, keys_out, igrad_out, wgrad,
+    tok, cot, sv, keys, igrad, in_s,
     te, wf0, wf1, wst, gs, gr, gx0, gx1, xr1, xr2, gy, yr, g1r, hx, xr3, pz, pr, qz, qr, acc, wn,
     pz_s, pz_r, px_s, px_r, py_s, py_r, pc_s, pc_r, ru_s, ru_r, rx_s, rx_r, rc_s, rc_r,
     sz_s, sz_r, sc_s, sc_r,
@@ -72,12 +74,19 @@
     z_partners = [(d, rel) for d in range(NZ) for rel in (0, 1) if (d, rel) != (0, 0)]
     z_partners.sort(key=lambda t: -min(t[0], NZ - t[0]))
 
+    loads = [
+        pltpu.make_async_copy(src, dst, in_s.at[i])
+        for i, (src, dst) in enumerate(((sv_in, sv), (tok_in, tok), (cot_in, cot)))
+    ]
+    for one in loads:
+        one.start()
+
     barrier = pltpu.get_barrier_semaphore()
     count = 0
     for d, rel in z_partners:
         pl.semaphore_signal(barrier, inc=1, device_id=dev(dz=d, core=o if rel else c), device_id_type=MESH)
         count += 1
-    for d in range(1, NY):
+    for d in (1, 2, 6, 7):
         pl.semaphore_signal(barrier, inc=1, device_id=dev(dy=d), device_id_type=MESH)
         count += 1
     for d in range(1, NX):
@@ -90,55 +99,18 @@
     factor = jnp.sum(jnp.where(hit, ps[...], 0.0), axis=1, keepdims=True)
     pz[...] = (dot(one_hot(hit), pv[...]) * factor).astype(BF).reshape(2, 16, 128)
 
-    pl.semaphore_wait(barrier, count)
-
-    for d, rel in z_partners:
-        to = o if rel else c
-        at = d * 2 + rel
-        send(pz.at[to], pr.at[z, c], pz_s.at[at], pz_r.at[at], dev(dz=d, core=to))
-    pr[z, c] = pz[c]
-
+    loads[0].wait()
     hit = iota((SEC, 342), 1) == iota((SEC, 342), 0) - (6 * nd) % 16
-    factor = jnp.sum(jnp.where(hit, sc[...], 0.0), axis=1, keepdims=True)
+    factor = jnp.sum(jnp.where(hit, sc[...][None, :], 0.0), axis=1, keepdims=True)
     wst[nd] = (dot(one_hot(hit), sv[...]) * factor).astype(BF)
-
-    def sec_part(n, piece):
-        return wst.at[n, pl.ds(0, SEC_A)] if piece == 0 else wst.at[n, pl.ds(SEC_A, SEC - SEC_A)]
-
-    def sec_node(side, hop):
-        return ((zl - hop + 6) % 6 if side == 0 else (zl + hop) % 6) * 2
-
-    def sec_index(side, hop, piece):
-        return side * 6 + (hop - 1) * 2 + piece
-
-    def sec_send(side, hop, piece):
-        part = sec_part(sec_node(side, hop - 1) + c, piece)
-        at = sec_index(side, hop, piece)
-        send(part, part, sz_s.at[at], sz_r.at[at], dev(dz=1 if side == 0 else NZ - 1))
-
-    def sec_cross(side, hop, piece):
-        part = sec_part(sec_node(side, hop) + c, piece)
-        at = sec_index(side, hop, piece) if hop else 12 + piece
-        send(part, part, sc_s.at[at], sc_r.at[at], dev(core=o))
-
-    def sec_arrive(hop, order):
-        for side in (0, 1):
-            piece = side ^ order
-            at = sec_index(side, hop, piece)
-            landed(sec_part(sec_node(side, hop) + c, piece), sz_s.at[at], sz_r.at[at])
-            if hop == 1 or (hop == 2 and order == 0):
-                sec_send(side, hop + 1, piece)
-            sec_cross(side, hop, piece)
-
-    for order in (0, 1):
-        for side in (0, 1):
-            sec_send(side, 1, side ^ order)
 
     d = iota((1, SLAB), 1)
     xx = (d >= ROWS).astype(jnp.int32) + (d >= 2 * ROWS).astype(jnp.int32) + (d >= 3 * ROWS).astype(jnp.int32)
     j = d - ROWS * xx
     low = jnp.where(j < 66, 66 * xx + j, -100000)
     high = jnp.where((j >= 66) & (j < 132), 66 * xx + j - 66, -100000)
+    loads[1].wait()
+    loads[2].wait()
     for yy in range(NY):
         total = None
         for start, base in ((264 * yy, low), (2112 + 264 * yy, high)):
@@ -155,30 +127,51 @@
         out = lax.dot_general(rows, part, (((0,), (0,)), ((), ())), preferred_element_type=F32)
         return out.reshape(NX, ROWS, HALF)
 
-    def give(k):
+    for k in range(8):
         gs[k] = grad(k, o).astype(BF)
+
+    pl.semaphore_wait(barrier, count)
+
+    for d, rel in z_partners:
+        to = o if rel else c
+        at = d * 2 + rel
+        send(pz.at[to], pr.at[z, c], pz_s.at[at], pz_r.at[at], dev(dz=d, core=to))
+    pr[z, c] = pz[c]
+
+    for k in range(8):
         send(gs.at[k], gr.at[k], gc_s.at[k], gc_r.at[k], dev(core=o))
 
-    for k in range(4):
-        give(k)
-
-    for d, rel in z_partners:
-        at = d * 2 + rel
-        landed(pr.at[(z - d + NZ) % NZ, o if rel else c], pz_s.at[at], pz_r.at[at])
-    packets = pr[...].reshape(NZ * 32, 128)
-    k = iota((ROWS, NZ * 32), 1)
-    r = iota((ROWS, NZ * 32), 0)
-    wf1[c, x, 0] = dot(one_hot(line_of(k, 1) == r), packets).astype(BF)
-    wf0[c, 0, x] = dot(one_hot(line_of(k, 0) == r), packets).astype(BF)
-    for d in (4, 3, 5, 2, 6, 1, 7):
-        send(wf1.at[c, x, 0], wf1.at[c, x, NY - d], ru_s.at[d], ru_r.at[d], dev(dy=d))
-    for d in (2, 1, 3):
-        own = wf0.at[c, 0, x]
-        send(own, own, px_s.at[d], px_r.at[d], dev(dx=d))
-
-    for k in range(4, 8):
-        give(k)
-    sec_arrive(1, 0)
+    def sec_part(n, piece):
+        return wst.at[n, pl.ds(0, SEC_A)] if piece == 0 else wst.at[n, pl.ds(SEC_A, SEC - SEC_A)]
+
+    def sec_node(side, hop):
+        return ((zl - hop + 6) % 6 if side == 0 else (zl + hop) % 6) * 2
+
+    def sec_index(side, hop, piece):
+        return side * 6 + (hop - 1) * 2 + piece
+
+    def sec_send(side, hop, piece):
+        part = sec_part(sec_node(side, hop - 1) + c, piece)
+        at = sec_index(side, hop, piece)
+        send(part, part, sz_s.at[at], sz_r.at[at], dev(dz=1 if side == 0 else NZ - 1))
+
+    def sec_cross(side, hop, piece):
+        part = sec_part(sec_node(side, hop) + c, piece)
+        at = sec_index(side, hop, piece) if hop else 12 + piece
+        send(part, part, sc_s.at[at], sc_r.at[at], dev(core=o))
+
+    def sec_arrive(hop, order):
+        for side in (0, 1):
+            piece = side ^ order
+            at = sec_index(side, hop, piece)
+            landed(sec_part(sec_node(side, hop) + c, piece), sz_s.at[at], sz_r.at[at])
+            if hop == 1 or (hop == 2 and order == 0):
+                sec_send(side, hop + 1, piece)
+            sec_cross(side, hop, piece)
+
+    for order in (0, 1):
+        for side in (0, 1):
+            sec_send(side, 1, side ^ order)
 
     def pri_part(core, side, hop, piece):
         return wf0.at[core, (NY - hop) % NY if side == 0 else hop, pl.ds(2 * piece, 2)]
@@ -214,6 +207,34 @@
         for piece in (0, 1):
             pri_cross(0, 0, piece)
 
+    def near_slot(side, far):
+        r = NY - 1 - far if side == 0 else 1 + far
+        if far < 3:
+            return wf1.at[c, x, r]
+        return wf1.at[c, x, r, pl.ds(0, CUT) if side == 0 else pl.ds(CUT, ROWS - CUT)]
+
+    def near_send(side, far):
+        slot = near_slot(side, far)
+        if far < 2:
+            src = wf1.at[c, x, 0]
+        elif far == 2:
+            src = near_slot(side, 1)
+        else:
+            src = wf1.at[c, x, 6 if side == 0 else 2, pl.ds(0, CUT) if side == 0 else pl.ds(CUT, ROWS - CUT)]
+        at = side * 4 + far
+        step = 2 if far in (1, 3) else 1
+        send(src, slot, ru_s.at[at], ru_r.at[at], dev(dy=step if side == 0 else NY - step))
+
+    def near_landed(side, far):
+        at = side * 4 + far
+        landed(near_slot(side, far), ru_s.at[at], ru_r.at[at])
+
+    def alt_mid():
+        for side in (0, 1):
+            near_landed(side, 1)
+            near_send(side, 3)
+            near_send(side, 2)
+
     def alt_part(core, side, hop, piece):
         xx = (x - hop + NX) % NX if side == 0 else (x + hop) % NX
         return wf1.at[core, xx, pl.ds(4 * piece, 4)]
@@ -241,8 +262,9 @@
             alt_cross(side, hop, piece)
 
     def alt_turn():
-        for d in range(1, NY):
-            landed(wf1.at[c, x, NY - d], ru_s.at[d], ru_r.at[d])
+        for far in (0, 2, 3):
+            for side in (0, 1):
+                near_landed(side, far)
         for order in (0, 1):
             for side in (0, 1):
                 alt_send(side, 1, side ^ order)
@@ -303,50 +325,82 @@
         x_send(side, 0, p)
         x_send(1 - side, 1, p)
 
+    def pri_line():
+        for d, rel in z_partners:
+            at = d * 2 + rel
+            landed(pr.at[(z - d + NZ) % NZ, o if rel else c], pz_s.at[at], pz_r.at[at])
+        packets = pr[...].reshape(NZ * 32, 128)
+        k = iota((ROWS, NZ * 32), 1)
+        r = iota((ROWS, NZ * 32), 0)
+        wf1[c, x, 0] = dot(one_hot(line_of(k, 1) == r), packets).astype(BF)
+        wf0[c, 0, x] = dot(one_hot(line_of(k, 0) == r), packets).astype(BF)
+        for far in (1, 0):
+            for side in (0, 1):
+                near_send(side, far)
+        for d in (2, 1, 3):
+            own = wf0.at[c, 0, x]
+            send(own, own, px_s.at[d], px_r.at[d], dev(dx=d))
+
     own_half(0)
     own_half(1)
-    pri_turn()
+    pri_line()
     own_half(2)
     own_half(3)
+    sec_arrive(1, 0)
+    pri_turn()
+    y_turn(0, 1, 0)
+    y_turn(1, 1, 1)
+    x_turn(0)
+    x_turn(1)
+    alt_mid()
     sec_arrive(1, 1)
     for piece in (0, 1):
         sec_cross(0, 0, piece)
-    x_turn(0)
-    x_turn(1)
-    y_turn(0, 1, 0)
-    y_turn(1, 1, 1)
-    alt_turn()
-    pri_arrive(1, 0)
-    sec_arrive(2, 0)
     y_turn(0, 2, 1)
     y_turn(1, 2, 0)
     x_turn(2)
     x_turn(3)
-    pri_arrive(1, 1)
+    pri_arrive(1, 0)
+    alt_turn()
     y_turn(0, 2, 0)
     y_turn(1, 2, 1)
-    pri_arrive(2, 0)
+    sec_arrive(2, 0)
+    pri_arrive(1, 1)
     y_turn(0, 3, 1)
     y_turn(1, 3, 0)
-    sec_arrive(2, 1)
-    pri_arrive(2, 1)
-    alt_arrive(1, 0)
+    pri_arrive(2, 0)
     y_turn(0, 3, 0)
     y_turn(1, 3, 1)
+
+    def fold_send(side, far, r):
+        at = side * 4 + far
+        k = PLACE[r]
+        step = 2 if far in (1, 3) else 1
+        part = pl.ds(0, ROWS) if far < 3 else (pl.ds(0, CUT) if side == 0 else pl.ds(CUT, ROWS - CUT))
+        send(gy.at[k, part], yr.at[at, part], gy_s.at[at], gy_r.at[at], dev(dy=step if side == 0 else NY - step))
+
+    def fold_landed(side, far):
+        at = side * 4 + far
+        part = pl.ds(0, ROWS) if far < 3 else (pl.ds(0, CUT) if side == 0 else pl.ds(CUT, ROWS - CUT))
+        landed(yr.at[at, part], gy_s.at[at], gy_r.at[at])
 
     for p in (0, 1, 2, 3):
         for side in (0, 1):
             at = side * 6 + 2 + p
             landed(xr2.at[side, pl.ds(2 * p, 2)], gx_s.at[at], gx_r.at[at])
         for k in (2 * p, 2 * p + 1):
-            mine = (gx0[x, k].astype(F32) + xr2[0, k].astype(F32) + xr2[1, k].astype(F32)).astype(BF)
-            if RING[k]:
-                gy[k] = mine
-                send(gy.at[k], yr.at[k], gy_s.at[k], gy_r.at[k], dev(dy=RING[k]))
-            else:
-                yr[k] = mine
-    pri_arrive(3, 0)
-    sec_arrive(3, 0)
+            gy[k] = (gx0[x, k].astype(F32) + xr2[0, k].astype(F32) + xr2[1, k].astype(F32)).astype(BF)
+            r = RING[k]
+            if r == 4:
+                fold_send(0, 3, 4)
+                fold_send(1, 3, 4)
+            elif r in (3, 5):
+                fold_send(0 if r == 3 else 1, 2, r)
+            elif r in (1, 7):
+                fold_send(0 if r == 1 else 1, 0, r)
+    pri_arrive(2, 1)
+    sec_arrive(2, 1)
+    alt_arrive(1, 0)
 
     for piece in (1, 0):
         for side in (0, 1):
@@ -356,16 +410,27 @@
     for d in (2, 1, 3):
         send(hx.at[(x + d) % NX], xr3.at[d], hx_s.at[d], hx_r.at[d], dev(dx=d))
     xr3[0] = hx[x]
+
+    for side in (0, 1):
+        fold_landed(side, 2)
+        fold_landed(side, 3)
+        k = PLACE[2 if side == 0 else 6]
+        gy[k] = (gy[k].astype(F32) + yr[side * 4 + 2].astype(F32)).astype(BF)
+        part = pl.ds(0, CUT) if side == 0 else pl.ds(CUT, ROWS - CUT)
+        gy[k, part] = (gy[k, part].astype(F32) + yr[side * 4 + 3, part].astype(F32)).astype(BF)
+        fold_send(side, 1, 2 if side == 0 else 6)
+    pri_arrive(3, 0)
+    sec_arrive(3, 0)
     alt_arrive(1, 1)
     pri_arrive(3, 1)
     alt_arrive(2, 0)
     pri_arrive(4, 0)
 
-    for k in range(7):
-        landed(yr.at[k], gy_s.at[k], gy_r.at[k])
-    line0 = yr[0].astype(F32)
-    for k in range(1, NY):
-        line0 = line0 + yr[k].astype(F32)
+    line0 = gy[PLACE[0]].astype(F32)
+    for far in (0, 1):
+        for side in (0, 1):
+            fold_landed(side, far)
+            line0 = line0 + yr[side * 4 + far].astype(F32)
     for d in range(1, NX):
         landed(xr3.at[d], hx_s.at[d], hx_r.at[d])
     line1 = xr3[0].astype(F32)
@@ -402,6 +467,9 @@
         igrad[:, 512 * i:512 * i + 512] = lax.dot_general(
             cot[...], wn[512 * i:512 * i + 512], (((1,), (1,)), ((), ())), preferred_element_type=F32
         ).astype(BF)
+
+    stores = [pltpu.make_async_copy(igrad, igrad_out, in_s.at[3])]
+    stores[0].start()
 
     for piece in (0, 1):
         at = 16 + piece
@@ -426,6 +494,9 @@
             total = part if total is None else total + part
         keys[:, HALF * core:HALF * core + HALF] = total.astype(BF)
 
+    stores.append(pltpu.make_async_copy(keys, keys_out, in_s.at[4]))
+    stores[1].start()
+
     for d, rel in z_partners:
         at = d * 2 + rel
         landed(qr.at[(z - d + NZ) % NZ, o if rel else c], gz_s.at[at], gz_r.at[at])
@@ -442,6 +513,8 @@
     scale = 1.0 / jnp.sqrt(F32(128 * NX * NY * NZ * 2))
     wgrad[...] = acc[:22] * scale
 
+    for one in stores:
+        one.wait()
     for one in sent:
         one.wait_send()
 
@@ -449,6 +522,7 @@
 def local(tokens, cotangent, prim_values, prim_scales, sec_values, sec_scales):
     dma = pltpu.SemaphoreType.DMA
     vmem = pl.BlockSpec(memory_space=pltpu.VMEM)
+    hbm = pl.BlockSpec(memory_space=pltpu.HBM)
     groups = [24, 4, 16, 18, 8, 8, 10, 12, 14, 8, 12, 8, 16, 4, 24]
     return pl.pallas_call(
         kernel,
@@ -458,9 +532,15 @@
             jax.ShapeDtypeStruct((128, 4096), BF),
             jax.ShapeDtypeStruct((22, 128), F32),
         ),
-        in_specs=[vmem] * 6,
-        out_specs=(vmem, vmem, vmem),
+        in_specs=[hbm, hbm, vmem, vmem, hbm, vmem],
+        out_specs=(hbm, hbm, vmem),
         scratch_shapes=[
+            pltpu.VMEM((128, 4096), BF),
+            pltpu.VMEM((128, 512), BF),
+            pltpu.VMEM((342, 512), BF),
+            pltpu.VMEM((128, 512), BF),
+            pltpu.VMEM((128, 4096), BF),
+            dma((5,)),
             pltpu.VMEM((NY, 128, SLAB), BF),
             pltpu.VMEM((2, NY, NX, ROWS, LANES), BF),
             pltpu.VMEM((2, NX, NY, ROWS, LANES), BF),
@@ -485,9 +565,9 @@
         ]
         + [dma((n,)) for n in groups for _ in (0, 1)],
         compiler_params=pltpu.CompilerParams(
-            collective_id=0, has_side_effects=True, vmem_limit_bytes=52 * 2**20
+            collective_id=0, has_side_effects=True, vmem_limit_bytes=60 * 2**20
         ),
-    )(tokens, cotangent, prim_values, prim_scales.reshape(1, -1), sec_values, sec_scales.reshape(1, -1))
+    )(tokens, cotangent, prim_values, prim_scales.reshape(1, -1), sec_values, sec_scales)
 
 
 def solution(mesh):

time: 80.5 us -> 74.1 us (0.920)
  Pallas kernels: 74 us -> 68.7 us
  local copies, waits for them, and re-layouts: 5.5 us -> 4.47 us
    pallas_call x1, Pallas kernels: 74 us -> 68.7 us  [local(): pl.pallas_call(kernel, name='sharded_projection', out_shape=(jax.ShapeDty...]
    unnamed x11 -> x5, local copies, waits for them, and re-layouts: 4.81 us -> 4.47 us
where the time goes in v3:
time: 74.1 us; the launch traced here: 73.8 us
  Pallas kernels  68.7 us (93%)
  local copies, waits for them, and re-layouts  4.47 us (6%)
    pallas_call x1, Pallas kernels, local(): pl.pallas_call(kernel, name='sharded_projection', out_shape=(jax.ShapeDty...  68.7 us
    unnamed x5, local copies, waits for them, and re-layouts  4.47 us

profile of v3, /device:TPU:1, one launch (start us, length us, event | category | flops | bytes accessed | tf_op | source)
XLA Modules:
  0.0 73.8 jit_solution(14269450993583407556)
XLA Ops:
  0.6 68.7 %sharded_projection.1 = (bf16[128,512]{1,0:T(8,128)(2,1)}, bf16[128,4096]{1,0:T(8,128)(2,1)}, f32[22,128]{1,0:T(8,128)}) custom-call(bf16[128,4096]{1,0:T(8,128)(2,1)} %tok_in.1, bf16[128,512]{1,0:T(8,128)(2,1)} %cot_in.1, bf16[22,128]{1,0:T(8,128)(2,1)} %pv.1, f32[1,22]{1,0:T(1,128)} %bitcast.1, bf16[342,512]{1,0:T(8,128)(2,1)} %sv_in.1, f32[342]{0:T(512)} %sc.1), custom_call_target="tpu_custom_call" | custom-call | tf_op jit(solution)/shard_map/sharded_projection/pallas_call | solution.py:527
  69.4 1.6 %copy.12 = bf16[128,512]{1,0:T(8,128)(2,1)} copy(bf16[128,512]{1,0:T(8,128)(2,1)} %get-tuple-element.6) | data formatting | bytes 262144
  70.9 0.0 copy-start
  70.9 2.3 %copy.13 = bf16[128,4096]{1,0:T(8,128)(2,1)} copy(bf16[128,4096]{1,0:T(8,128)(2,1)} %get-tuple-element.7) | data formatting | bytes 2097152
  73.2 0.0 copy-done
  73.2 0.6 copy.14
Async XLA Ops:
  70.9 2.3 %copy-start = (f32[22,128]{1,0:T(8,128)S(1)}, f32[22,128]{1,0:T(8,128)}, u32[]{:S(2)}) copy-start(f32[22,128]{1,0:T(8,128)} %get-tuple-element.8) | copy-start | bytes 33796

commit v4 on v3

--- a/solution.py
+++ b/solution.py
@@ -14,6 +14,9 @@
 HALF = 256
 SLAB = NX * ROWS
 CUT = 64
+ROWS0 = 80
+ROWS1 = 2 * ROWS - ROWS0
+CUT1 = 96
 LANES = 128
 SEC = 368
 SEC_A = 192
@@ -127,8 +130,9 @@
         out = lax.dot_general(rows, part, (((0,), (0,)), ((), ())), preferred_element_type=F32)
         return out.reshape(NX, ROWS, HALF)
 
-    for k in range(8):
+    def give(k):
         gs[k] = grad(k, o).astype(BF)
+        send(gs.at[k], gr.at[k], gc_s.at[k], gc_r.at[k], dev(core=o))
 
     pl.semaphore_wait(barrier, count)
 
@@ -138,8 +142,8 @@
         send(pz.at[to], pr.at[z, c], pz_s.at[at], pz_r.at[at], dev(dz=d, core=to))
     pr[z, c] = pz[c]
 
-    for k in range(8):
-        send(gs.at[k], gr.at[k], gc_s.at[k], gc_r.at[k], dev(core=o))
+    for k in (0, 1):
+        give(k)
 
     def sec_part(n, piece):
         return wst.at[n, pl.ds(0, SEC_A)] if piece == 0 else wst.at[n, pl.ds(SEC_A, SEC - SEC_A)]
@@ -172,6 +176,8 @@
     for order in (0, 1):
         for side in (0, 1):
             sec_send(side, 1, side ^ order)
+    for k in range(2, 8):
+        give(k)
 
     def pri_part(core, side, hop, piece):
         return wf0.at[core, (NY - hop) % NY if side == 0 else hop, pl.ds(2 * piece, 2)]
@@ -211,7 +217,7 @@
         r = NY - 1 - far if side == 0 else 1 + far
         if far < 3:
             return wf1.at[c, x, r]
-        return wf1.at[c, x, r, pl.ds(0, CUT) if side == 0 else pl.ds(CUT, ROWS - CUT)]
+        return wf1.at[c, x, r, pl.ds(0, CUT1) if side == 0 else pl.ds(CUT1, ROWS1 - CUT1)]
 
     def near_send(side, far):
         slot = near_slot(side, far)
@@ -220,7 +226,7 @@
         elif far == 2:
             src = near_slot(side, 1)
         else:
-            src = wf1.at[c, x, 6 if side == 0 else 2, pl.ds(0, CUT) if side == 0 else pl.ds(CUT, ROWS - CUT)]
+            src = wf1.at[c, x, 6 if side == 0 else 2, pl.ds(0, CUT1) if side == 0 else pl.ds(CUT1, ROWS1 - CUT1)]
         at = side * 4 + far
         step = 2 if far in (1, 3) else 1
         send(src, slot, ru_s.at[at], ru_r.at[at], dev(dy=step if side == 0 else NY - step))
@@ -330,10 +336,12 @@
             at = d * 2 + rel
             landed(pr.at[(z - d + NZ) % NZ, o if rel else c], pz_s.at[at], pz_r.at[at])
         packets = pr[...].reshape(NZ * 32, 128)
-        k = iota((ROWS, NZ * 32), 1)
+        k = iota((1, NZ * 32), 1)
         r = iota((ROWS, NZ * 32), 0)
-        wf1[c, x, 0] = dot(one_hot(line_of(k, 1) == r), packets).astype(BF)
-        wf0[c, 0, x] = dot(one_hot(line_of(k, 0) == r), packets).astype(BF)
+        slab = dot(one_hot(line_of(k, 0) == r), packets).astype(BF)
+        wf1[c, x, 0, pl.ds(0, ROWS)] = dot(one_hot(line_of(k, 1) == r), packets).astype(BF)
+        wf1[c, x, 0, pl.ds(ROWS, ROWS - ROWS0)] = slab[ROWS0:]
+        wf0[c, 0, x] = slab[:ROWS0]
         for far in (1, 0):
             for side in (0, 1):
                 near_send(side, far)
@@ -436,7 +444,7 @@
     line1 = xr3[0].astype(F32)
     for d in range(1, NX):
         line1 = line1 + xr3[d].astype(F32)
-    k = iota((NZ * 32, ROWS), 0)
+    k = iota((NZ * 32, 1), 0)
     r = iota((NZ * 32, ROWS), 1)
     packets = dot(one_hot(line_of(k, 0) == r), line0.astype(BF)) + dot(one_hot(line_of(k, 1) == r), line1.astype(BF))
     qz[...] = packets.astype(BF).reshape(NZ, 2, 16, 128)
@@ -489,13 +497,18 @@
     for core in (0, 1):
         total = None
         for r in range(NY):
-            w = jnp.concatenate([wf0[core, r].reshape(SLAB, LANES), wf1[core, :, r].reshape(SLAB, LANES)], axis=1)
+            first = jnp.concatenate([wf0[core, r], wf1[core, :, r, pl.ds(ROWS, ROWS - ROWS0)]], axis=1)
+            second = wf1[core, :, r, pl.ds(0, ROWS)]
+            w = jnp.concatenate([first.reshape(SLAB, LANES), second.reshape(SLAB, LANES)], axis=1)
             part = dot(te[(y + r) % NY], w)
             total = part if total is None else total + part
         keys[:, HALF * core:HALF * core + HALF] = total.astype(BF)
 
     stores.append(pltpu.make_async_copy(keys, keys_out, in_s.at[4]))
     stores[1].start()
+
+    for one in sent:
+        one.wait_send()
 
     for d, rel in z_partners:
         at = d * 2 + rel
@@ -515,8 +528,18 @@
 
     for one in stores:
         one.wait()
-    for one in sent:
-        one.wait_send()
+
+
+def hand_over(keys, igrad, wgrad, keys_out, igrad_out, wgrad_out, out_s):
+    copies = [pltpu.make_async_copy(wgrad, wgrad_out, out_s.at[0])]
+    copies.append(pltpu.make_async_copy(keys, keys_out, out_s.at[1]))
+    for i in range(8):
+        part = pl.ds(16 * i, 16)
+        copies.append(pltpu.make_async_copy(igrad.at[part], igrad_out.at[part], out_s.at[2 + i]))
+    for one in copies:
+        one.start()
+    for one in copies:
+        one.wait()
 
 
 def local(tokens, cotangent, prim_values, prim_scales, sec_values, sec_scales):
@@ -524,14 +547,15 @@
     vmem = pl.BlockSpec(memory_space=pltpu.VMEM)
     hbm = pl.BlockSpec(memory_space=pltpu.HBM)
     groups = [24, 4, 16, 18, 8, 8, 10, 12, 14, 8, 12, 8, 16, 4, 24]
-    return pl.pallas_call(
+    shapes = (
+        jax.ShapeDtypeStruct((128, 512), BF),
+        jax.ShapeDtypeStruct((128, 4096), BF),
+        jax.ShapeDtypeStruct((22, 128), F32),
+    )
+    results = pl.pallas_call(
         kernel,
         name="sharded_projection",
-        out_shape=(
-            jax.ShapeDtypeStruct((128, 512), BF),
-            jax.ShapeDtypeStruct((128, 4096), BF),
-            jax.ShapeDtypeStruct((22, 128), F32),
-        ),
+        out_shape=shapes,
         in_specs=[hbm, hbm, vmem, vmem, hbm, vmem],
         out_specs=(hbm, hbm, vmem),
         scratch_shapes=[
@@ -542,8 +566,8 @@
             pltpu.VMEM((128, 4096), BF),
             dma((5,)),
             pltpu.VMEM((NY, 128, SLAB), BF),
-            pltpu.VMEM((2, NY, NX, ROWS, LANES), BF),
-            pltpu.VMEM((2, NX, NY, ROWS, LANES), BF),
+            pltpu.VMEM((2, NY, NX, ROWS0, LANES), BF),
+            pltpu.VMEM((2, NX, NY, ROWS1, LANES), BF),
             pltpu.VMEM((12, SEC, 512), BF),
             pltpu.VMEM((NY, NX, ROWS, HALF), BF),
             pltpu.VMEM((NY, NX, ROWS, HALF), BF),
@@ -568,6 +592,15 @@
             collective_id=0, has_side_effects=True, vmem_limit_bytes=60 * 2**20
         ),
     )(tokens, cotangent, prim_values, prim_scales.reshape(1, -1), sec_values, sec_scales)
+    return pl.pallas_call(
+        hand_over,
+        name="results",
+        out_shape=shapes,
+        in_specs=[hbm] * 3,
+        out_specs=(hbm, hbm, hbm),
+        scratch_shapes=[dma((10,))],
+        compiler_params=pltpu.CompilerParams(vmem_limit_bytes=60 * 2**20),
+    )(*results)
 
 
 def solution(mesh):

time: 74.1 us -> 104 us (1.40)
  Pallas kernels: 68.7 us -> 103 us
  local copies, waits for them, and re-layouts: 4.47 us -> 0 us
    pallas_call x1 -> x2, Pallas kernels: 68.7 us -> 103 us  [the longest x1 65.9 us: local(): pl.pallas_call(kernel, name='sharded_projection', out_shape=shapes, in_sp...]
    unnamed x5 -> x0, local copies, waits for them, and re-layouts: 4.47 us -> none
where the time goes in v4:
time: 104 us
  Pallas kernels  103 us (99%)
    pallas_call x1, Pallas kernels, local(): pl.pallas_call(kernel, name='sharded_projection', out_shape=shapes, in_sp...  65.9 us
    pallas_call x1, Pallas kernels, local(): pl.pallas_call(hand_over, name='results', out_shape=shapes, in_specs=[hbm...  37.3 us

profile of v4, /device:TPU:1, one launch (start us, length us, event | category | flops | bytes accessed | tf_op | source)
XLA Modules:
  0.0 103.8 jit_solution(13699337789689928674)
XLA Ops:
  0.6 65.9 %sharded_projection.1 = (bf16[128,512]{1,0:T(8,128)(2,1)}, bf16[128,4096]{1,0:T(8,128)(2,1)}, f32[22,128]{1,0:T(8,128)}) custom-call(bf16[128,4096]{1,0:T(8,128)(2,1)} %tok_in.1, bf16[128,512]{1,0:T(8,128)(2,1)} %cot_in.1, bf16[22,128]{1,0:T(8,128)(2,1)} %pv.1, f32[1,22]{1,0:T(1,128)} %bitcast.1, bf16[342,512]{1,0:T(8,128)(2,1)} %sv_in.1, f32[342]{0:T(512)} %sc.1), custom_call_target="tpu_custom_call" | custom-call | tf_op jit(solution)/shard_map/sharded_projection/pallas_call | solution.py:555
  66.5 37.3 %results.1 = (bf16[128,512]{1,0:T(8,128)(2,1)}, bf16[128,4096]{1,0:T(8,128)(2,1)}, f32[22,128]{1,0:T(8,128)}) custom-call(bf16[128,512]{1,0:T(8,128)(2,1)} %get-tuple-element.6.keys, bf16[128,4096]{1,0:T(8,128)(2,1)} %get-tuple-element.7.igrad, f32[22,128]{1,0:T(8,128)} %get-tuple-element.8.wgrad), custom_call_target="tpu_custom_call" | custom-call | tf_op jit(solution)/shard_map/results/pallas_call | solution.py:595

commit v5 on v4

--- a/solution.py
+++ b/solution.py
@@ -374,12 +374,6 @@
     y_turn(1, 2, 1)
     sec_arrive(2, 0)
     pri_arrive(1, 1)
-    y_turn(0, 3, 1)
-    y_turn(1, 3, 0)
-    pri_arrive(2, 0)
-    y_turn(0, 3, 0)
-    y_turn(1, 3, 1)
-
     def fold_send(side, far, r):
         at = side * 4 + far
         k = PLACE[r]
@@ -406,18 +400,11 @@
                 fold_send(0 if r == 3 else 1, 2, r)
             elif r in (1, 7):
                 fold_send(0 if r == 1 else 1, 0, r)
-    pri_arrive(2, 1)
-    sec_arrive(2, 1)
-    alt_arrive(1, 0)
-
-    for piece in (1, 0):
-        for side in (0, 1):
-            at = y_at(side, 4, piece)
-            landed(g1r.at[side, 3, pl.ds(2 * piece, 2)], hy_s.at[at], hy_r.at[at])
-    hx[...] = (gx1[PLACE[0]].astype(F32) + g1r[0, 3].astype(F32) + g1r[1, 3].astype(F32)).astype(BF)
-    for d in (2, 1, 3):
-        send(hx.at[(x + d) % NX], xr3.at[d], hx_s.at[d], hx_r.at[d], dev(dx=d))
-    xr3[0] = hx[x]
+    y_turn(0, 3, 1)
+    y_turn(1, 3, 0)
+    pri_arrive(2, 0)
+    y_turn(0, 3, 0)
+    y_turn(1, 3, 1)
 
     for side in (0, 1):
         fold_landed(side, 2)
@@ -427,12 +414,21 @@
         part = pl.ds(0, CUT) if side == 0 else pl.ds(CUT, ROWS - CUT)
         gy[k, part] = (gy[k, part].astype(F32) + yr[side * 4 + 3, part].astype(F32)).astype(BF)
         fold_send(side, 1, 2 if side == 0 else 6)
+
+    pri_arrive(2, 1)
+    sec_arrive(2, 1)
+    alt_arrive(1, 0)
+
+    for piece in (1, 0):
+        for side in (0, 1):
+            at = y_at(side, 4, piece)
+            landed(g1r.at[side, 3, pl.ds(2 * piece, 2)], hy_s.at[at], hy_r.at[at])
+    hx[...] = (gx1[PLACE[0]].astype(F32) + g1r[0, 3].astype(F32) + g1r[1, 3].astype(F32)).astype(BF)
+    for d in (2, 1, 3):
+        send(hx.at[(x + d) % NX], xr3.at[d], hx_s.at[d], hx_r.at[d], dev(dx=d))
+    xr3[0] = hx[x]
+
     pri_arrive(3, 0)
-    sec_arrive(3, 0)
-    alt_arrive(1, 1)
-    pri_arrive(3, 1)
-    alt_arrive(2, 0)
-    pri_arrive(4, 0)
 
     line0 = gy[PLACE[0]].astype(F32)
     for far in (0, 1):
@@ -453,6 +449,12 @@
         at = d * 2 + rel
         send(qz.at[(z + d) % NZ, to], qr.at[z, c], gz_s.at[at], gz_r.at[at], dev(dz=d, core=to))
     qr[z, c] = qz[z, c]
+
+    sec_arrive(3, 0)
+    alt_arrive(1, 1)
+    pri_arrive(3, 1)
+    alt_arrive(2, 0)
+    pri_arrive(4, 0)
 
     for piece in (0, 1):
         landed(sec_part(zl * 2 + o, piece), sc_s.at[12 + piece], sc_r.at[12 + piece])
@@ -530,15 +532,19 @@
         one.wait()
 
 
-def hand_over(keys, igrad, wgrad, keys_out, igrad_out, wgrad_out, out_s):
-    copies = [pltpu.make_async_copy(wgrad, wgrad_out, out_s.at[0])]
-    copies.append(pltpu.make_async_copy(keys, keys_out, out_s.at[1]))
-    for i in range(8):
-        part = pl.ds(16 * i, 16)
-        copies.append(pltpu.make_async_copy(igrad.at[part], igrad_out.at[part], out_s.at[2 + i]))
-    for one in copies:
+def hand_over(keys, igrad, wgrad, keys_out, igrad_out, wgrad_out, keys_at, igrad_at, wgrad_at, in_s, out_s):
+    moves = [(keys, keys_at, keys_out), (wgrad, wgrad_at, wgrad_out)]
+    for i in range(4):
+        part = pl.ds(32 * i, 32)
+        moves.append((igrad.at[part], igrad_at.at[part], igrad_out.at[part]))
+    loads = [pltpu.make_async_copy(src, mid, in_s.at[i]) for i, (src, mid, dst) in enumerate(moves)]
+    stores = [pltpu.make_async_copy(mid, dst, out_s.at[i]) for i, (src, mid, dst) in enumerate(moves)]
+    for one in loads:
         one.start()
-    for one in copies:
+    for load, store in zip(loads, stores):
+        load.wait()
+        store.start()
+    for one in stores:
         one.wait()
 
 
@@ -598,7 +604,13 @@
         out_shape=shapes,
         in_specs=[hbm] * 3,
         out_specs=(hbm, hbm, hbm),
-        scratch_shapes=[dma((10,))],
+        scratch_shapes=[
+            pltpu.VMEM((128, 512), BF),
+            pltpu.VMEM((128, 4096), BF),
+            pltpu.VMEM((22, 128), F32),
+            dma((6,)),
+            dma((6,)),
+        ],
         compiler_params=pltpu.CompilerParams(vmem_limit_bytes=60 * 2**20),
     )(*results)
 

time: 104 us -> 68.8 us (0.66)
  Pallas kernels: 103 us -> 68 us
    pallas_call x1, Pallas kernels: 37.3 us -> 2.1 us  [local(): pl.pallas_call(hand_over, name='results', out_shape=shapes, in_specs=[hbm...]
where the time goes in v5:
time: 68.8 us; the launch traced here: 68.6 us
  Pallas kernels  68 us (99%)
    pallas_call x1, Pallas kernels, local(): pl.pallas_call(kernel, name='sharded_projection', out_shape=shapes, in_sp...  65.9 us
    pallas_call x1, Pallas kernels, local(): pl.pallas_call(hand_over, name='results', out_shape=shapes, in_specs=[hbm...  2.1 us

profile of v5, /device:TPU:1, one launch (start us, length us, event | category | flops | bytes accessed | tf_op | source)
XLA Modules:
  0.0 68.6 jit_solution(16099656913433173163)
XLA Ops:
  0.6 65.9 %sharded_projection.1 = (bf16[128,512]{1,0:T(8,128)(2,1)}, bf16[128,4096]{1,0:T(8,128)(2,1)}, f32[22,128]{1,0:T(8,128)}) custom-call(bf16[128,4096]{1,0:T(8,128)(2,1)} %tok_in.1, bf16[128,512]{1,0:T(8,128)(2,1)} %cot_in.1, bf16[22,128]{1,0:T(8,128)(2,1)} %pv.1, f32[1,22]{1,0:T(1,128)} %bitcast.1, bf16[342,512]{1,0:T(8,128)(2,1)} %sv_in.1, f32[342]{0:T(512)} %sc.1), custom_call_target="tpu_custom_call" | custom-call | tf_op jit(solution)/shard_map/sharded_projection/pallas_call | solution.py:561
  66.5 2.1 %results.1 = (bf16[128,512]{1,0:T(8,128)(2,1)}, bf16[128,4096]{1,0:T(8,128)(2,1)}, f32[22,128]{1,0:T(8,128)}) custom-call(bf16[128,512]{1,0:T(8,128)(2,1)} %get-tuple-element.6.keys, bf16[128,4096]{1,0:T(8,128)(2,1)} %get-tuple-element.7.igrad, f32[22,128]{1,0:T(8,128)} %get-tuple-element.8.wgrad), custom_call_target="tpu_custom_call" | custom-call | tf_op jit(solution)/shard_map/results/pallas_call | solution.py:601
